TPU v7x, 32 devices: a whole 2x2x4 slice. The times are simulated.
32 devices in a mesh: dp: 4 (over x, core), seq: 8 (over z, y).
Axes of the slice: x: 2, y: 2, z: 4, core: 2. Of those that a mesh axis runs over, the one named last changes fastest.
Arguments:
- patches: bfloat16 [50176, 768], P(('dp', 'seq')), may hold values from -6 to 6
- keep_index: int32 [1024, 49], P('dp'), may hold values from 0 to 195, as said below
- ln1_gain: float32 [768], replicated, may hold values from 0.25 to 1.75
- ln1_shift: float32 [768], replicated, may hold values from -1.75 to 1.75
- w_qkv: bfloat16 [768, 2304], replicated, may hold values from -0.21875 to 0.21875
- q_bias: float32 [768], replicated, may hold values from -3 to 3
- v_bias: float32 [768], replicated, may hold values from -3 to 3
- w_out: bfloat16 [768, 768], replicated, may hold values from -0.875 to 0.875
- out_bias: float32 [768], replicated, may hold values from -1.75 to 1.75
- ln2_gain: float32 [768], replicated, may hold values from 0.25 to 1.75
- ln2_shift: float32 [768], replicated, may hold values from -1.75 to 1.75
- w_fc1: bfloat16 [768, 3072], replicated, may hold values from -0.21875 to 0.21875
- fc1_bias: float32 [3072], replicated, may hold values from -3 to 3
- w_fc2: bfloat16 [3072, 768], replicated, may hold values from -0.109375 to 0.109375
- fc2_bias: float32 [768], replicated, may hold values from -1.75 to 1.75
- w_embed: bfloat16 [768, 512], replicated, may hold values from -0.21875 to 0.21875
- embed_bias: float32 [512], replicated, may hold values from -1.75 to 1.75
- mask_token: float32 [512], replicated, may hold values from -6 to 6
- decoder_grad: bfloat16 [200704, 512], P(('dp', 'seq')), may hold values from -6 to 6
Outputs:
- decoder_input: bfloat16 [200704, 512], P(('dp', 'seq'))
- patches_grad: bfloat16 [50176, 768], P(('dp', 'seq'))
- ln1_gain_grad: float32 [768], P('seq')
- ln1_shift_grad: float32 [768], P('seq')
- w_qkv_grad: float32 [768, 2304], P('seq')
- q_bias_grad: float32 [768], P('seq')
- v_bias_grad: float32 [768], P('seq')
- w_out_grad: float32 [768, 768], P('seq')
- out_bias_grad: float32 [768], P('seq')
- ln2_gain_grad: float32 [768], P('seq')
- ln2_shift_grad: float32 [768], P('seq')
- w_fc1_grad: float32 [768, 3072], P('seq')
- fc1_bias_grad: float32 [3072], P('seq')
- w_fc2_grad: float32 [3072, 768], P('seq')
- fc2_bias_grad: float32 [768], P('seq')
- w_embed_grad: float32 [768, 512], P('seq')
- embed_bias_grad: float32 [512], P('seq')
- mask_token_grad: float32 [512], P('seq')
Inputs may be any that keep to these rules, and one draw needn't show every extreme that they name: `keep_index`: each image's 49 kept positions are distinct and ascending. In a group, decoder device s holds rows s * 32 * 196 up to (s + 1) * 32 * 196 of the group's (position * 256 + image) rows. Of one image, at most 12 kept positions fall on one decoder device and at least one on each; in each group one decoder device gets exactly 12 from every image of the group.
All inputs are finite; a program needn't handle non-finite values.
Results may differ from a plain program's by a relative error of at most 0.019.
Values may be sent and summed in bfloat16 or wider, within the bound.
A program may use at most 256 MiB of HBM per device.

v0:
```python
import jax
import jax.numpy as jnp
from jax import lax
from jax.sharding import PartitionSpec as P

D = 768
HEADS = 12
HEAD = 64
DEC = 512
PATCHES = 196


EPSILON = 1e-06


def layer_norm(values, gain_vec, shift_vec):
    row_mean = jnp.mean(values, axis=-1, keepdims=True)
    centered = values - row_mean
    row_var = jnp.mean(centered * centered, axis=-1, keepdims=True)
    return centered * lax.rsqrt(row_var + EPSILON) * gain_vec + shift_vec


def gelu_exact(values):
    return jax.nn.gelu(values, approximate=False)


def soft_rows(scores):
    return jax.nn.softmax(scores, axis=-1)


def local(
    patches,
    keep_index,
    ln1_gain,
    ln1_shift,
    w_qkv,
    q_bias,
    v_bias,
    w_out,
    out_bias,
    ln2_gain,
    ln2_shift,
    w_fc1,
    fc1_bias,
    w_fc2,
    fc2_bias,
    w_embed,
    embed_bias,
    mask_token,
    decoder_grad,
):
    seq_count = lax.axis_size("seq")
    seq_pos = lax.axis_index("seq")
    group_imgs, keep_len = keep_index.shape
    img_dev = group_imgs // seq_count
    slot_count = 2 * keep_len // seq_count
    dev_rows = img_dev * PATCHES
    total_slots = img_dev * seq_count * slot_count
    own_rows = img_dev * keep_len
    image_ids = jnp.arange(group_imgs, dtype=jnp.int32)[:, None]
    grid_rows = keep_index * group_imgs + image_ids
    owner_dev = grid_rows // dev_rows
    owner_row = grid_rows % dev_rows
    lower_cnt = jnp.sum((owner_dev[:, None, :] < owner_dev[:, :, None]).astype(jnp.int32), axis=2)
    slot_rank = jnp.arange(keep_len, dtype=jnp.int32)[None, :] - lower_cnt
    own_owner = lax.dynamic_slice_in_dim(owner_dev, seq_pos * img_dev, img_dev, 0)
    own_rank = lax.dynamic_slice_in_dim(slot_rank, seq_pos * img_dev, img_dev, 0)
    send_slot = (
        (jnp.arange(img_dev, dtype=jnp.int32)[:, None] * seq_count + own_owner) * slot_count
        + own_rank
    ).reshape(-1)
    slot_source = (
        jnp.full((total_slots,), own_rows, jnp.int32)
        .at[send_slot]
        .set(jnp.arange(own_rows, dtype=jnp.int32))
    )
    slot_used = slot_source < own_rows
    source_idx = jnp.minimum(slot_source, own_rows - 1)
    is_mine = owner_dev == seq_pos
    slot_match = is_mine[:, None, :] & (
        slot_rank[:, None, :] == jnp.arange(slot_count, dtype=jnp.int32)[None, :, None]
    )
    slot_row = jnp.sum(jnp.where(slot_match, owner_row[:, None, :] + 1, 0), axis=2) - 1
    slot_row = slot_row.reshape(seq_count, img_dev, slot_count).transpose(1, 0, 2).reshape(-1)
    recv_used = slot_row >= 0
    row_source = (
        jnp.full((dev_rows,), total_slots, jnp.int32)
        .at[jnp.where(recv_used, slot_row, dev_rows)]
        .set(jnp.arange(total_slots, dtype=jnp.int32), mode="drop")
    )
    covered = row_source < total_slots
    recv_idx = jnp.minimum(row_source, total_slots - 1)
    pick_row = jnp.maximum(slot_row, 0)
    tok_rows = patches.astype(jnp.float32)
    first_f, first_pull = jax.vjp(layer_norm, tok_rows, ln1_gain, ln1_shift)
    first_in = first_f.astype(jnp.bfloat16)
    zero_bias = jnp.zeros_like(q_bias)
    qkv_rows = (
        jnp.dot(first_in, w_qkv, preferred_element_type=jnp.float32)
        + jnp.concatenate([q_bias, zero_bias, v_bias])
    ).astype(jnp.bfloat16)
    qkv_heads = qkv_rows.reshape(img_dev, keep_len, 3, HEADS, HEAD)
    queries = qkv_heads[:, :, 0]
    key_part = qkv_heads[:, :, 1]
    value_part = qkv_heads[:, :, 2]
    scale_qk = HEAD ** (-0.5)
    scores = (
        jnp.einsum("bqhd,bkhd->bhqk", queries, key_part, preferred_element_type=jnp.float32)
        * scale_qk
    )
    attn_probs, soft_pull = jax.vjp(soft_rows, scores)
    probs_in = attn_probs.astype(jnp.bfloat16)
    attended = (
        jnp.einsum("bhqk,bkhd->bqhd", probs_in, value_part, preferred_element_type=jnp.float32)
        .reshape(own_rows, D)
        .astype(jnp.bfloat16)
    )
    hidden = tok_rows + (jnp.dot(attended, w_out, preferred_element_type=jnp.float32) + out_bias)
    second_f, second_pull = jax.vjp(layer_norm, hidden, ln2_gain, ln2_shift)
    second_in = second_f.astype(jnp.bfloat16)
    inner_pre = jnp.dot(second_in, w_fc1, preferred_element_type=jnp.float32) + fc1_bias
    active_f, gelu_pull = jax.vjp(gelu_exact, inner_pre)
    active = active_f.astype(jnp.bfloat16)
    block_out = hidden + (jnp.dot(active, w_fc2, preferred_element_type=jnp.float32) + fc2_bias)
    block_in = block_out.astype(jnp.bfloat16)
    embedded = (jnp.dot(block_in, w_embed, preferred_element_type=jnp.float32) + embed_bias).astype(
        jnp.bfloat16
    )
    send_rows = jnp.where(
        slot_used[:, None], embedded[source_idx], jnp.zeros((), jnp.bfloat16)
    ).reshape(img_dev, seq_count, slot_count, DEC)
    arrived = lax.all_to_all(send_rows, "seq", split_axis=1, concat_axis=1, tiled=True).reshape(
        total_slots, DEC
    )
    mask_low = mask_token.astype(jnp.bfloat16)
    decoder_input = jnp.where(covered[:, None], arrived[recv_idx], mask_low[None, :])
    mask_grad = jnp.sum(jnp.where(covered[:, None], 0.0, decoder_grad.astype(jnp.float32)), axis=0)
    grad_slots = jnp.where(
        recv_used[:, None], decoder_grad[pick_row], jnp.zeros((), jnp.bfloat16)
    ).reshape(img_dev, seq_count, slot_count, DEC)
    returned = lax.all_to_all(grad_slots, "seq", split_axis=1, concat_axis=1, tiled=True).reshape(
        total_slots, DEC
    )
    embed_grad = returned[send_slot]
    w_embed_grad = jnp.einsum("nd,ne->de", block_in, embed_grad, preferred_element_type=jnp.float32)
    embed_bias_grad = jnp.sum(embed_grad.astype(jnp.float32), axis=0)
    out_grad = jnp.einsum("ne,de->nd", embed_grad, w_embed, preferred_element_type=jnp.float32)
    two_grad = out_grad.astype(jnp.bfloat16)
    fc2_bias_grad = jnp.sum(two_grad.astype(jnp.float32), axis=0)
    w_fc2_grad = jnp.einsum("nf,nd->fd", active, two_grad, preferred_element_type=jnp.float32)
    active_grad = jnp.einsum("nd,fd->nf", two_grad, w_fc2, preferred_element_type=jnp.float32)
    inner_grad = gelu_pull(active_grad)[0].astype(jnp.bfloat16)
    fc1_bias_grad = jnp.sum(inner_grad.astype(jnp.float32), axis=0)
    w_fc1_grad = jnp.einsum("nd,nf->df", second_in, inner_grad, preferred_element_type=jnp.float32)
    second_grad = jnp.einsum("nf,df->nd", inner_grad, w_fc1, preferred_element_type=jnp.float32)
    hidden_part, ln2_gain_grad, ln2_shift_grad = second_pull(second_grad)
    hidden_grad = out_grad + hidden_part
    branch_grad = hidden_grad.astype(jnp.bfloat16)
    out_bias_grad = jnp.sum(branch_grad.astype(jnp.float32), axis=0)
    w_out_grad = jnp.einsum("nd,ne->de", attended, branch_grad, preferred_element_type=jnp.float32)
    attended_grad = (
        jnp.einsum("ne,de->nd", branch_grad, w_out, preferred_element_type=jnp.float32)
        .astype(jnp.bfloat16)
        .reshape(img_dev, keep_len, HEADS, HEAD)
    )
    probs_grad = jnp.einsum(
        "bqhd,bkhd->bhqk", attended_grad, value_part, preferred_element_type=jnp.float32
    )
    value_grad = jnp.einsum(
        "bhqk,bqhd->bkhd", probs_in, attended_grad, preferred_element_type=jnp.float32
    )
    score_grad = soft_pull(probs_grad)[0].astype(jnp.bfloat16)
    query_grad = (
        jnp.einsum("bhqk,bkhd->bqhd", score_grad, key_part, preferred_element_type=jnp.float32)
        * scale_qk
    )
    key_grad = (
        jnp.einsum("bhqk,bqhd->bkhd", score_grad, queries, preferred_element_type=jnp.float32)
        * scale_qk
    )
    qkv_grad = (
        jnp.stack([query_grad, key_grad, value_grad], axis=2)
        .reshape(own_rows, 3 * D)
        .astype(jnp.bfloat16)
    )
    qkv_sums = jnp.sum(qkv_grad.astype(jnp.float32), axis=0)
    q_bias_grad = qkv_sums[:D]
    v_bias_grad = qkv_sums[2 * D :]
    w_qkv_grad = jnp.einsum("nd,nc->dc", first_in, qkv_grad, preferred_element_type=jnp.float32)
    first_grad = jnp.einsum("nc,dc->nd", qkv_grad, w_qkv, preferred_element_type=jnp.float32)
    rows_part, ln1_gain_grad, ln1_shift_grad = first_pull(first_grad)
    patches_grad = (hidden_grad + rows_part).astype(jnp.bfloat16)
    (
        ln1_gain_share,
        ln1_shift_share,
        w_qkv_share,
        q_bias_share,
        v_bias_share,
        w_out_share,
        out_bias_share,
        ln2_gain_share,
        ln2_shift_share,
        w_fc1_share,
        fc1_bias_share,
        w_fc2_share,
        fc2_bias_share,
        w_embed_share,
        embed_bias_share,
        mask_share,
    ) = (
        lax.psum_scatter(
            ln1_gain_grad.astype(jnp.bfloat16), "seq", scatter_dimension=0, tiled=True
        ).astype(jnp.float32),
        lax.psum_scatter(
            ln1_shift_grad.astype(jnp.bfloat16), "seq", scatter_dimension=0, tiled=True
        ).astype(jnp.float32),
        lax.psum_scatter(
            w_qkv_grad.astype(jnp.bfloat16), "seq", scatter_dimension=0, tiled=True
        ).astype(jnp.float32),
        lax.psum_scatter(
            q_bias_grad.astype(jnp.bfloat16), "seq", scatter_dimension=0, tiled=True
        ).astype(jnp.float32),
        lax.psum_scatter(
            v_bias_grad.astype(jnp.bfloat16), "seq", scatter_dimension=0, tiled=True
        ).astype(jnp.float32),
        lax.psum_scatter(
            w_out_grad.astype(jnp.bfloat16), "seq", scatter_dimension=0, tiled=True
        ).astype(jnp.float32),
        lax.psum_scatter(
            out_bias_grad.astype(jnp.bfloat16), "seq", scatter_dimension=0, tiled=True
        ).astype(jnp.float32),
        lax.psum_scatter(
            ln2_gain_grad.astype(jnp.bfloat16), "seq", scatter_dimension=0, tiled=True
        ).astype(jnp.float32),
        lax.psum_scatter(
            ln2_shift_grad.astype(jnp.bfloat16), "seq", scatter_dimension=0, tiled=True
        ).astype(jnp.float32),
        lax.psum_scatter(
            w_fc1_grad.astype(jnp.bfloat16), "seq", scatter_dimension=0, tiled=True
        ).astype(jnp.float32),
        lax.psum_scatter(
            fc1_bias_grad.astype(jnp.bfloat16), "seq", scatter_dimension=0, tiled=True
        ).astype(jnp.float32),
        lax.psum_scatter(
            w_fc2_grad.astype(jnp.bfloat16), "seq", scatter_dimension=0, tiled=True
        ).astype(jnp.float32),
        lax.psum_scatter(
            fc2_bias_grad.astype(jnp.bfloat16), "seq", scatter_dimension=0, tiled=True
        ).astype(jnp.float32),
        lax.psum_scatter(
            w_embed_grad.astype(jnp.bfloat16), "seq", scatter_dimension=0, tiled=True
        ).astype(jnp.float32),
        lax.psum_scatter(
            embed_bias_grad.astype(jnp.bfloat16), "seq", scatter_dimension=0, tiled=True
        ).astype(jnp.float32),
        lax.psum_scatter(
            mask_grad.astype(jnp.bfloat16), "seq", scatter_dimension=0, tiled=True
        ).astype(jnp.float32),
    )
    (
        ln1_gain_grad,
        ln1_shift_grad,
        w_qkv_grad,
        q_bias_grad,
        v_bias_grad,
        w_out_grad,
        out_bias_grad,
        ln2_gain_grad,
        ln2_shift_grad,
        w_fc1_grad,
        fc1_bias_grad,
        w_fc2_grad,
        fc2_bias_grad,
        w_embed_grad,
        embed_bias_grad,
        mask_grad,
    ) = (
        lax.psum(ln1_gain_share.astype(jnp.bfloat16), "dp").astype(jnp.float32),
        lax.psum(ln1_shift_share.astype(jnp.bfloat16), "dp").astype(jnp.float32),
        lax.psum(w_qkv_share.astype(jnp.bfloat16), "dp").astype(jnp.float32),
        lax.psum(q_bias_share.astype(jnp.bfloat16), "dp").astype(jnp.float32),
        lax.psum(v_bias_share.astype(jnp.bfloat16), "dp").astype(jnp.float32),
        lax.psum(w_out_share.astype(jnp.bfloat16), "dp").astype(jnp.float32),
        lax.psum(out_bias_share.astype(jnp.bfloat16), "dp").astype(jnp.float32),
        lax.psum(ln2_gain_share.astype(jnp.bfloat16), "dp").astype(jnp.float32),
        lax.psum(ln2_shift_share.astype(jnp.bfloat16), "dp").astype(jnp.float32),
        lax.psum(w_fc1_share.astype(jnp.bfloat16), "dp").astype(jnp.float32),
        lax.psum(fc1_bias_share.astype(jnp.bfloat16), "dp").astype(jnp.float32),
        lax.psum(w_fc2_share.astype(jnp.bfloat16), "dp").astype(jnp.float32),
        lax.psum(fc2_bias_share.astype(jnp.bfloat16), "dp").astype(jnp.float32),
        lax.psum(w_embed_share.astype(jnp.bfloat16), "dp").astype(jnp.float32),
        lax.psum(embed_bias_share.astype(jnp.bfloat16), "dp").astype(jnp.float32),
        lax.psum(mask_share.astype(jnp.bfloat16), "dp").astype(jnp.float32),
    )
    return (
        decoder_input,
        patches_grad,
        ln1_gain_grad,
        ln1_shift_grad,
        w_qkv_grad,
        q_bias_grad,
        v_bias_grad,
        w_out_grad,
        out_bias_grad,
        ln2_gain_grad,
        ln2_shift_grad,
        w_fc1_grad,
        fc1_bias_grad,
        w_fc2_grad,
        fc2_bias_grad,
        w_embed_grad,
        embed_bias_grad,
        mask_grad,
    )


def solution(mesh):
    placed = (
        P(("dp", "seq"), None),
        P("dp", None),
        P(),
        P(),
        P(),
        P(),
        P(),
        P(),
        P(),
        P(),
        P(),
        P(),
        P(),
        P(),
        P(),
        P(),
        P(),
        P(),
        P(("dp", "seq"), None),
    )
    return jax.shard_map(
        local,
        mesh=mesh,
        in_specs=placed,
        out_specs=(
            P(("dp", "seq"), None),
            P(("dp", "seq"), None),
            P("seq"),
            P("seq"),
            P("seq", None),
            P("seq"),
            P("seq"),
            P("seq", None),
            P("seq"),
            P("seq"),
            P("seq"),
            P("seq", None),
            P("seq"),
            P("seq", None),
            P("seq"),
            P("seq", None),
            P("seq"),
            P("seq"),
        ),
        check_vma=False,
    )
```

profile of v0, /device:TPU:0, one launch (start us, length us, event | category | flops | bytes accessed | tf_op | source)
XLA Modules:
  0.0 912.1 jit_solution(205790038591235800)
XLA Ops:
  16.4 16.9 %gather_fusion.2 = bf16[3072,512]{1,0:T(8,128)(2,1)} fusion(bf16[6272,512]{1,0:T(8,128)(2,1)} %param.37, s32[3072]{0:T(1024)S(1)} %broadcast_clamp_fusion), kind=kCustom, calls=%fused_computation.2 | custom fusion | bytes 6303744 | tf_op jit(solution)/shard_map/gather | solution.py:139
  33.3 6.2 gather.20
  46.4 7.4 all-to-all-start.1
  59.9 8.5 add_convert_fusion.1
  68.4 22.5 %reshape.253 = bf16[32,49,3,12,64]{4,3,2,1,0:T(8,128)(2,1)} reshape(bf16[1568,2304]{1,0:T(8,128)(2,1)} %add_convert_fusion.1) | data formatting | bytes 14450688 | tf_op jit(solution)/shard_map/reshape | solution.py:102
  90.8 13.0 %fusion.58 = (bf16[32,49,1,12,64]{4,3,2,1,0:T(8,128)(2,1)}, bf16[32,49,1,12,64]{4,3,2,1,0:T(8,128)(2,1)}, bf16[32,49,1,12,64]{4,3,2,1,0:T(8,128)(2,1)}) fusion(bf16[32,49,3,12,64]{4,3,2,1,0:T(8,128)(2,1)} %reshape.253), kind=kLoop, calls=%fused_computation.139 | loop fusion | bytes 14450688 | tf_op jit(solution)/shard_map/slice | solution.py:104
  103.9 11.9 %fusion.25 = f32[32,12,49,49]{2,3,1,0:T(8,128)} fusion(bf16[32,49,1,12,64]{4,3,2,1,0:T(8,128)(2,1)} %get-tuple-element.63, bf16[32,49,1,12,64]{4,3,2,1,0:T(8,128)(2,1)} %get-tuple-element.62), kind=kOutput, calls=%fused_computation.70 | convolution fusion | flops 118013952 | bytes 8504832 | tf_op jit(solution)/shard_map/bqhd,bkhd->bhqk/dot_general | solution.py:108
  115.7 14.7 %fusion.60 = (f32[32,12,49]{2,1,0:T(8,128)S(1)}, f32[32,12,49,49]{2,3,1,0:T(8,128)}) fusion(f32[32,12,49,49]{2,3,1,0:T(8,128)} %fusion.25), kind=kOutput, calls=%fused_computation.141 | output fusion | flops 3687984 | bytes 7451136 | tf_op jit(solution)/shard_map/jvp()/sub | solution.py:28
  130.4 9.7 %convert_bitcast_fusion = bf16[32,49,12,64]{3,1,2,0:T(8,128)(2,1)} fusion(bf16[32,49,1,12,64]{4,3,2,1,0:T(8,128)(2,1)S(1)} %copy-done.5, f32[32,12,49,49]{2,3,1,0:T(8,128)} %get-tuple-element.71, f32[32,12,49]{2,1,0:T(8,128)S(1)} %get-tuple-element.70), kind=kOutput, calls=%fused_computation.48 | convolution fusion | flops 121062144 | bytes 8580096 | tf_op jit(solution)/shard_map/bhqk,bkhd->bqhd/dot_general | solution.py:114
  140.1 6.3 copy.93
  146.4 9.1 convert_element_type.204
  162.9 54.5 %multiply_convert_fusion = (bf16[1568,3072]{1,0:T(8,128)(2,1)}, f32[1568,3072]{1,0:T(8,128)}, f32[1568,3072]{1,0:T(8,128)}) fusion(f32[3072]{0:T(1024)S(1)} %copy-done.40, bf16[768,3072]{1,0:T(8,128)(2,1)} %param.30, f32[1568,768]{1,0:T(8,128)S(1)} %get-tuple-element.73, f32[768]{0:T(1024)S(1)} %copy-done.44, f32[768]{0:T(1024)S(1)} %copy-done.37, ...), kind=kOutput, calls=%fused_computation.11 | convolution fusion | flops 7722688512 | bytes 57735424 | tf_op jit(solution)/shard_map/dot_general | solution.py:121
  225.3 13.8 %add_convert_fusion.3 = bf16[1568,768]{1,0:T(8,128)(2,1)} fusion(f32[1568,768]{1,0:T(8,128)} %copy-done.7, bf16[1568,3072]{1,0:T(8,128)(2,1)} %get-tuple-element.60, bf16[3072,768]{1,0:T(8,128)(2,1)} %param.32, f32[768]{0:T(1024)} %param.33), kind=kOutput, calls=%fused_computation.64 | convolution fusion | flops 7402364928 | bytes 21580800 | tf_op jit(solution)/shard_map/dot_general | solution.py:124
  239.1 5.8 copy.98
  244.9 6.2 reshape.255
  251.1 8.5 gather_fusion.3
  264.9 27.7 %fusion.62 = (bf16[3072]{0:T(1024)(128)(2,1)}, bf16[1568,3072]{1,0:T(8,128)(2,1)}) fusion(f32[1568,3072]{1,0:T(8,128)} %get-tuple-element.61, bf16[3072,768]{1,0:T(8,128)(2,1)} %param.32, f32[1568,768]{1,0:T(8,128)} %fusion.63, f32[1568,3072]{1,0:T(8,128)} %get-tuple-element.74, f32[3072]{0:T(1024)S(1)} %copy-done.41), kind=kOutput, calls=%fused_computation.143 | convolution fusion | flops 7477023744 | bytes 57722880 | tf_op jit(solution)/shard_map/nd,fd->nf/dot_general | solution.py:151
  292.6 16.3 %multiply_reduce_fusion.2 = (bf16[768]{0:T(1024)(128)(2,1)}, f32[1568]{0:T(1024)S(1)}, bf16[768]{0:T(1024)(128)(2,1)}, f32[1568,768]{1,0:T(8,128)S(1)}) fusion(f32[1568,768]{1,0:T(8,128)} %copy-done.7, f32[1568]{0:T(1024)S(1)} %fusion.41, f32[1568]{0:T(1024)S(1)} %broadcast_multiply_fusion, f32[768]{0:T(1024)S(1)} %copy-done.38, ...), kind=kOutput, calls=%fused_computation.60 | convolution fusion | flops 7408382976 | bytes 24011136 | tf_op jit(solution)/shard_map/nf,df->nd/dot_general | solution.py:155
  320.5 8.3 reshape.256
  328.8 13.0 %multiply_reduce_fusion = (f32[32,12,49]{2,1,0:T(8,128)S(1)}, f32[32,12,49,49]{2,3,1,0:T(8,128)}) fusion(f32[32,12,49,49]{2,3,1,0:T(8,128)} %get-tuple-element.71, f32[32,12,49]{2,1,0:T(8,128)} %multiply_divide_fusion, bf16[32,49,1,12,64]{4,3,2,1,0:T(8,128)(2,1)} %get-tuple-element.64, bf16[32,49,12,64]{3,2,1,0:T(8,128)(2,1)} %reshape.256), kind=kOutput, calls=%fused_computation.30 | convolution fusion | flops 120761088 | bytes 12343296 | tf_op jit(solution)/shard_map/bqhd,bkhd->bhqk/dot_general | solution.py:166
  341.9 11.7 %multiply_convert_fusion.1 = bf16[32,12,49,49]{2,3,1,0:T(8,128)(2,1)} fusion(f32[32,12,49,49]{2,3,1,0:T(8,128)} %get-tuple-element.71, f32[32,12,49,49]{2,3,1,0:T(8,128)} %get-tuple-element.77, f32[32,12,49]{2,1,0:T(8,128)S(1)} %neg.22, f32[32,12,49]{2,1,0:T(8,128)S(1)} %copy-done.10), kind=kLoop, calls=%fused_computation.29 | loop fusion | flops 3687936 | bytes 9370368 | tf_op jit(solution)/shard_map/convert_element_type | solution.py:172
  353.6 9.9 %multiply_bitcast_fusion.1 = bf16[32,49,1,12,64]{4,1,3,0,2:T(8,128)(2,1)} fusion(bf16[32,12,49,49]{2,3,1,0:T(8,128)(2,1)} %multiply_convert_fusion.1, bf16[32,49,1,12,64]{4,3,2,1,0:T(8,128)(2,1)} %get-tuple-element.62), kind=kOutput, calls=%fused_computation.28 | convolution fusion | flops 120422400 | bytes 6660864 | tf_op jit(solution)/shard_map/bhqk,bkhd->bqhd/dot_general | solution.py:174
  363.5 9.8 %multiply_bitcast_fusion = bf16[32,49,1,12,64]{4,1,3,0,2:T(8,128)(2,1)} fusion(bf16[32,12,49,49]{2,3,1,0:T(8,128)(2,1)} %multiply_convert_fusion.1, bf16[32,49,1,12,64]{4,3,2,1,0:T(8,128)(2,1)} %get-tuple-element.63), kind=kOutput, calls=%fused_computation.27 | convolution fusion | flops 120422400 | bytes 6660864 | tf_op jit(solution)/shard_map/bhqk,bqhd->bkhd/dot_general | solution.py:178
  373.3 5.8 convolution_convert_fusion.4
  383.8 9.6 %fusion.30 = bf16[32,49,1,12,64]{4,1,3,0,2:T(8,128)(2,1)} fusion(bf16[32,49,12,64]{3,2,1,0:T(8,128)(2,1)} %reshape.256, f32[32,12,49,49]{2,3,1,0:T(8,128)} %get-tuple-element.71, f32[32,12,49]{2,1,0:T(8,128)} %copy-done.9), kind=kOutput, calls=%fused_computation.77 | convolution fusion | flops 119857920 | bytes 8580096 | tf_op jit(solution)/shard_map/bhqk,bqhd->bkhd/dot_general | solution.py:169
  393.5 10.9 %fusion.55 = (bf16[3,12,64]{2,1,0:T(8,128)(2,1)}, bf16[32,49,3,12,64]{4,1,3,0,2:T(8,128)(2,1)S(1)}) fusion(bf16[32,49,1,12,64]{4,1,3,0,2:T(8,128)(2,1)} %fusion.30, bf16[32,49,1,12,64]{4,1,3,0,2:T(8,128)(2,1)} %multiply_bitcast_fusion, bf16[32,49,1,12,64]{4,1,3,0,2:T(8,128)(2,1)} %multiply_bitcast_fusion.1), kind=kLoop, calls=%fused_computation.137 | loop fusion | flops 10835712 | bytes 14455296 | tf_op jit(solution)/shard_map/reduce_sum | solution.py:186
  404.3 9.6 %copy.102 = bf16[32,49,3,12,64]{4,3,2,1,0:T(8,128)(2,1)} copy(bf16[32,49,3,12,64]{4,1,3,0,2:T(8,128)(2,1)S(1)} %get-tuple-element.55) | data formatting | bytes 14450688 | tf_op jit(solution)/shard_map/convert_element_type | solution.py:184
  414.0 23.8 %convert_element_type.216 = bf16[1568,2304]{1,0:T(8,128)(2,1)} reshape(bf16[32,49,3,12,64]{4,3,2,1,0:T(8,128)(2,1)} %copy.102) | data formatting | bytes 14450688 | tf_op jit(solution)/shard_map/convert_element_type | solution.py:184
  437.8 12.0 %convolution_convert_fusion.1 = bf16[768,2304]{1,0:T(8,128)(2,1)} fusion(bf16[1568,2304]{1,0:T(8,128)(2,1)} %convert_element_type.216, bf16[1568,768]{1,0:T(8,128)(2,1)} %param.19, f32[768]{0:T(1024)} %param.22, f32[768]{0:T(1024)} %param.21, f32[1568]{0:T(1024)S(1)} %copy-done.21, f32[1568]{0:T(1024)S(1)} %copy-done.15), kind=kOutput, calls=%fused_computation.53 | convolution fusion | flops 5558059008 | bytes 13191424 | tf_op jit(solution)/shard_map/nd,nc->dc/dot_general | solution.py:189
  449.9 15.7 %convolution_convert_fusion.2 = bf16[768,3072]{1,0:T(8,128)(2,1)} fusion(bf16[1568,3072]{1,0:T(8,128)(2,1)} %get-tuple-element.80, f32[1568,768]{1,0:T(8,128)} %copy-done.7, f32[768]{0:T(1024)} %param.29, f32[768]{0:T(1024)} %param.28, f32[1568]{0:T(1024)} %copy-done.30, f32[1568]{0:T(1024)} %copy-done.22), kind=kOutput, calls=%fused_computation.54 | convolution fusion | flops 7407132672 | bytes 19187968 | tf_op jit(solution)/shard_map/nd,nf->df/dot_general | solution.py:154
  465.6 14.4 %convolution_convert_fusion = bf16[3072,768]{1,0:T(8,128)(2,1)} fusion(bf16[1568,3072]{1,0:T(8,128)(2,1)} %get-tuple-element.60, f32[1568,768]{1,0:T(8,128)} %fusion.63), kind=kOutput, calls=%fused_computation.52 | convolution fusion | flops 7402315776 | bytes 19169280 | tf_op jit(solution)/shard_map/nf,nd->fd/dot_general | solution.py:150
  480.6 9.5 %scatter_custom_fusion.1 = s32[3072]{0:T(1024)} fusion(s32[1568]{0:T(1024)} %copy-done.31, s32[1568]{0:T(1024)} %iota.29, s32[]{:T(128)} %constant.57.clone.1), kind=kCustom, calls=%fused_computation.123 | custom fusion | bytes 12800 | tf_op jit(solution)/shard_map/scatter | solution.py:75
  495.9 16.1 %gather_fusion = bf16[3072,512]{1,0:T(8,128)(2,1)} fusion(bf16[1568,512]{1,0:T(8,128)(2,1)} %add_convert_fusion.5, s32[3072]{0:T(1024)} %fusion.39), kind=kCustom, calls=%fused_computation | custom fusion | bytes 6303744 | tf_op jit(solution)/shard_map/gather | solution.py:130
  512.1 6.2 gather.17
  527.1 6.4 all-to-all-start
  538.7 12.5 %scatter_custom_fusion = s32[6272]{0:T(1024)} fusion(s32[3072]{0:T(1024)} %bitcast.70, s32[3072]{0:T(1024)} %iota.27, s32[]{:T(128)} %constant.50.clone.1), kind=kCustom, calls=%fused_computation.106 | custom fusion | bytes 25600 | tf_op jit(solution)/shard_map/scatter | solution.py:89
  553.9 5.8 select_reduce_fusion
  565.3 11.1 %fusion.52 = (bf16[768]{0:T(1024)(128)(2,1)}, f32[1568]{0:T(1024)S(1)}, f32[1568,768]{1,0:T(8,128)S(1)}) fusion(f32[768]{0:T(1024)} %param.21, f32[1568]{0:T(1024)S(1)} %copy-done.15, bf16[1568,768]{1,0:T(8,128)(2,1)} %param.19, bf16[1568,2304]{1,0:T(8,128)(2,1)} %convert_element_type.216, bf16[768,2304]{1,0:T(8,128)(2,1)S(1)} %copy-done), kind=kOutput, calls=%fused_computation.135 | convolution fusion | flops 5556286976 | bytes 18006784 | tf_op jit(solution)/shard_map/nc,dc->nd/dot_general | solution.py:190
  579.4 69.1 %all-reduce.11 = (bf16[768]{0:T(1024)(128)(2,1)}, bf16[768]{0:T(1024)(128)(2,1)}, bf16[768]{0:T(1024)(128)(2,1)}, bf16[768]{0:T(1024)(128)(2,1)S(1)}, bf16[768]{...) all-reduce(bf16[768]{0:T(1024)(128)(2,1)} %get-tuple-element.20, ...), channel_id=2, replica_groups=mesh['dp'=4,'seq'=8] {'seq'}, use_global_device_ids=true, to_apply=%region_16.17.clone | all-reduce | flops 10240 | bytes 40960
  660.3 7.1 all-reduce.12
  679.5 5.9 copy.95
  685.4 6.2 reshape.254
  691.7 21.4 %gather_fusion.1 = bf16[6272,512]{1,0:T(8,128)(2,1)} fusion(bf16[3072,512]{1,0:T(8,128)(2,1)} %reshape.254, s32[7168]{0:T(1024)} %pad_clamp_fusion), kind=kCustom, calls=%fused_computation.1 | custom fusion | bytes 12870144 | tf_op jit(solution)/shard_map/gather | solution.py:136
  713.7 7.9 broadcast_select_fusion
  721.6 25.4 %reduce-scatter.10.cloned.1.call-done = bf16[96,3072]{1,0:T(8,128)(2,1)} async-done(((bf16[768,3072]{1,0:T(8,128)(2,1)}), bf16[96,3072]{1,0:T(8,128)(2,1)}) %reduce-scatter.10.cloned.1.call-update) | async-done | bytes 589840 | tf_op jit(solution)/shard_map/reduce_scatter | solution.py:238
  747.1 99.0 %reduce-scatter.12.cloned.1.call-done = bf16[384,768]{1,0:T(8,128)(2,1)} async-done(((bf16[3072,768]{1,0:T(8,128)(2,1)}), bf16[384,768]{1,0:T(8,128)(2,1)}) %reduce-scatter.12.cloned.1.call-update) | async-done | bytes 589840 | tf_op jit(solution)/shard_map/reduce_scatter | solution.py:244
  846.1 8.5 add_convert_fusion.2
  854.6 42.4 %all-reduce.16.cloned.1.call-done = (bf16[96,2304]{1,0:T(8,128)(2,1)}, bf16[96,768]{1,0:T(8,128)(2,1)}, bf16[96,3072]{1,0:T(8,128)(2,1)}, bf16[384,768]{1,0:T(8,128)(2,1)}, bf16[96,512]{1,0:T(8,128)(2,1)}) async-done(((bf16[96,2304]{1,0:T(8,128)(2,1)}, bf16[96,768]{1,0:T(8,128)(2,1)}, bf16[96,3072]{1,0:T(8,128)(2,1)}, bf16[384,768]{1,0:T(8,128)(2,1)}, bf16[96,512]{1,0:T(8,128)(2,1)}), ...) | async-done | bytes 1867792 | tf_op jit(solution)/shard_map/psum | solution.py:280
  (193 shorter events, 121.0 us)
Async XLA Ops:
  7.2 52.7 %copy-start = (bf16[768,2304]{1,0:T(8,128)(2,1)S(1)}, bf16[768,2304]{1,0:T(8,128)(2,1)}, u32[]{:S(2)}) copy-start(bf16[768,2304]{1,0:T(8,128)(2,1)} %param.23) | copy-start | bytes 10616836
  8.2 0.6 copy-start.11
  10.2 0.6 copy-start.12
  33.3 6.2 copy-start.28
  46.4 12.9 %copy-start.35 = (f32[768]{0:T(1024)S(1)}, f32[768]{0:T(1024)}, u32[]{:S(2)}) copy-start(f32[768]{0:T(1024)} %param.25) | copy-start | bytes 9220
  46.4 12.9 %copy-start.36 = (f32[768]{0:T(1024)S(1)}, f32[768]{0:T(1024)}, u32[]{:S(2)}) copy-start(f32[768]{0:T(1024)} %param.24) | copy-start | bytes 9220
  46.4 13.5 %copy-start.33 = (f32[768]{0:T(1024)S(1)}, f32[768]{0:T(1024)}, u32[]{:S(2)}) copy-start(f32[768]{0:T(1024)} %param.21) | copy-start | bytes 9220
  46.4 13.5 %copy-start.43 = (f32[768]{0:T(1024)S(1)}, f32[768]{0:T(1024)}, u32[]{:S(2)}) copy-start(f32[768]{0:T(1024)} %param.22) | copy-start | bytes 9220
  46.4 192.7 %all-to-all-start.1 = ((bf16[32,8,12,512]{3,0,2,1:T(8,128)(2,1)}), bf16[32,8,12,512]{3,0,2,1:T(8,128)(2,1)}, u32[]{:S(2)}, u32[]{:S(2)}) async-start(bf16[32,8,12,512]{3,0,2,1:T(8,128)(2,1)} %copy.97), calls=%async_computation.1 | async-start | bytes 6291456 | tf_op jit(solution)/shard_map/all_to_all | solution.py:141
  53.8 667.8 %reduce-scatter.14.cloned.1.call-start = ((), (), s32[]{:S(2)}) async-start(), calls=%async_computation.11 | async-start | bytes 884736 | tf_op jit(solution)/shard_map/reduce_scatter | solution.py:250
  53.9 6.0 copy-start.3
  56.1 3.2 copy-start.14
  115.7 14.7 %copy-start.5 = (bf16[32,49,1,12,64]{4,3,2,1,0:T(8,128)(2,1)S(1)}, bf16[32,49,1,12,64]{4,3,2,1,0:T(8,128)(2,1)}, u32[]{:S(2)}) copy-start(bf16[32,49,1,12,64]{4,3,2,1,0:T(8,128)(2,1)} %get-tuple-element.64) | copy-start | bytes 7225348
  130.4 9.7 %copy-start.9 = (f32[32,12,49]{2,1,0:T(8,128)}, f32[32,12,49]{2,1,0:T(8,128)S(1)}, u32[]{:S(2)}) copy-start(f32[32,12,49]{2,1,0:T(8,128)S(1)} %get-tuple-element.70) | copy-start | bytes 225796
  146.4 9.1 copy-start.42
  160.7 2.2 copy-start.7
  160.7 2.2 copy-start.37
  160.7 2.2 copy-start.40
  160.7 2.2 copy-start.44
  160.7 148.3 %copy-start.22 = (f32[1568]{0:T(1024)}, f32[1568]{0:T(1024)S(1)}, u32[]{:S(2)}) copy-start(f32[1568]{0:T(1024)S(1)} %broadcast_multiply_fusion) | copy-start | bytes 18820
  162.9 146.1 %copy-start.30 = (f32[1568]{0:T(1024)}, f32[1568]{0:T(1024)S(1)}, u32[]{:S(2)}) copy-start(f32[1568]{0:T(1024)S(1)} %fusion.41) | copy-start | bytes 18820
  259.7 5.3 copy-start.41
  264.9 27.7 %copy-start.38 = (f32[768]{0:T(1024)S(1)}, f32[768]{0:T(1024)}, u32[]{:S(2)}) copy-start(f32[768]{0:T(1024)} %param.28) | copy-start | bytes 9220
  292.6 16.3 %copy-start.26 = (f32[1568]{0:T(1024)S(1)}, f32[1568]{0:T(1024)}, u32[]{:S(2)}) copy-start(f32[1568]{0:T(1024)} %copy-done.25) | copy-start | bytes 18820
  309.0 4.3 copy-start.1
  313.3 2.3 copy-start.2
  313.3 2.3 copy-start.17
  313.3 3.7 copy-start.39
  315.6 1.4 copy-start.8
  328.8 13.0 %copy-start.10 = (f32[32,12,49]{2,1,0:T(8,128)S(1)}, f32[32,12,49]{2,1,0:T(8,128)}, u32[]{:S(2)}) copy-start(f32[32,12,49]{2,1,0:T(8,128)} %copy-done.9) | copy-start | bytes 225796
  383.7 337.9 %reduce-scatter.8.cloned.1.call-start = ((), (), s32[]{:S(2)}) async-start(), calls=%async_computation.8 | async-start | bytes 1327104 | tf_op jit(solution)/shard_map/reduce_scatter | solution.py:226
  393.4 328.2 %reduce-scatter.6.cloned.1.call-start = ((), (), s32[]{:S(2)}) async-start(), calls=%async_computation.7 | async-start | bytes 3981312 | tf_op jit(solution)/shard_map/reduce_scatter | solution.py:217
  414.0 23.9 %copy-start.15 = (f32[1568]{0:T(1024)S(1)}, f32[1568]{0:T(1024)}, u32[]{:S(2)}) copy-start(f32[1568]{0:T(1024)} %copy-done.14) | copy-start | bytes 18820
  414.0 23.9 %copy-start.21 = (f32[1568]{0:T(1024)S(1)}, f32[1568]{0:T(1024)}, u32[]{:S(2)}) copy-start(f32[1568]{0:T(1024)} %copy-done.20) | copy-start | bytes 18820
  449.8 297.3 %reduce-scatter.10.cloned.1.call-start = ((), (), s32[]{:S(2)}) async-start(), calls=%async_computation.9 | async-start | bytes 5308416 | tf_op jit(solution)/shard_map/reduce_scatter | solution.py:238
  465.6 380.5 %reduce-scatter.12.cloned.1.call-start = ((), (), s32[]{:S(2)}) async-start(), calls=%async_computation.10 | async-start | bytes 5308416 | tf_op jit(solution)/shard_map/reduce_scatter | solution.py:244
  527.1 152.4 %all-to-all-start = ((bf16[32,8,12,512]{3,0,2,1:T(8,128)(2,1)}), bf16[32,8,12,512]{3,0,2,1:T(8,128)(2,1)}, u32[]{:S(2)}, u32[]{:S(2)}) async-start(bf16[32,8,12,512]{3,0,2,1:T(8,128)(2,1)} %copy.94), calls=%async_computation | async-start | bytes 6291456 | tf_op jit(solution)/shard_map/all_to_all | solution.py:132
  533.6 363.4 %all-reduce.16.cloned.1.call-start = ((), (), s32[]{:S(2)}) async-start(), calls=%async_computation.12 | async-start | bytes 3735552 | tf_op jit(solution)/shard_map/psum | solution.py:280
  551.2 8.6 copy-start.29
  565.3 11.1 %copy-start.24 = (f32[1568]{0:T(1024)S(1)}, f32[1568]{0:T(1024)}, u32[]{:S(2)}) copy-start(f32[1568]{0:T(1024)} %copy-done.23) | copy-start | bytes 18820
  565.3 11.1 %copy-start.4 = (bf16[1568,768]{1,0:T(8,128)(2,1)S(1)}, bf16[1568,768]{1,0:T(8,128)(2,1)}, u32[]{:S(2)}) copy-start(bf16[1568,768]{1,0:T(8,128)(2,1)} %param.19) | copy-start | bytes 7225348
  565.3 11.1 %copy-start.34 = (f32[768]{0:T(1024)S(1)}, f32[768]{0:T(1024)}, u32[]{:S(2)}) copy-start(f32[768]{0:T(1024)} %param.21) | copy-start | bytes 9220
  576.4 3.0 copy-start.6
  576.4 3.0 copy-start.19
  691.7 21.4 %copy-start.32 = (f32[1568]{0:T(1024)S(1)}, f32[1568]{0:T(1024)}, u32[]{:S(2)}) copy-start(f32[1568]{0:T(1024)} %get-tuple-element.21) | copy-start | bytes 18820
  713.7 132.4 %copy-start.18 = (f32[1568]{0:T(1024)S(1)}, f32[1568]{0:T(1024)}, u32[]{:S(2)}) copy-start(f32[1568]{0:T(1024)} %copy-done.17) | copy-start | bytes 18820
  897.0 6.4 copy-start.13
  897.0 7.1 copy-start.16
  (5 other events, 3.0 us)
Sparse Core Ops, SparseCore 0:
  383.9 63.8 reduce-scatter.13
  452.1 62.9 reduce-scatter.7
  519.2 128.8 reduce-scatter.5
  652.0 95.0 reduce-scatter.9
  751.0 95.0 reduce-scatter.11
  848.8 48.1 all-reduce.15
where the time goes:
time: 925 us; the launch traced here: 912 us
  matrix products  267 us (29%)
  local copies, waits for them, and re-layouts  254 us (27%)
  waiting for transfers between devices  167 us (18%)
  other arithmetic  117 us (13%)
  blocking collectives  76.2 us (8%)
  between operations  17 us (2%)
  starting transfers between devices  14.1 us (2%)
    reduce_scatter x1, waiting for transfers between devices, local(): lax.psum_scatter(w_fc2_grad.astype(jnp.bfloat16), 'seq', scatter_dimensio...  99 us
    unnamed x1, blocking collectives  69.1 us
    dot_general x1, matrix products, local(): jnp.dot(second_in, w_fc1, preferred_element_type=jnp.float32) + fc1_bias  54.5 us
    psum x1, waiting for transfers between devices, local(): lax.psum(w_qkv_share.astype(jnp.bfloat16), 'dp').astype(jnp.float32)  42.4 us
    convert_element_type x2, local copies, waits for them, and re-layouts, local(): qkv_grad = jnp.stack([query_grad, key_grad, value_grad], axis=2).reshape(...  33.5 us
    dot_general x1, matrix products, local(): jnp.einsum('nd,fd->nf', two_grad, w_fc2, preferred_element_type=jnp.float32)  27.7 us
    reduce_scatter x1, waiting for transfers between devices, local(): lax.psum_scatter(w_fc1_grad.astype(jnp.bfloat16), 'seq', scatter_dimensio...  25.4 us
    gather x2, local copies, waits for them, and re-layouts, local(): decoder_grad[pick_row]  23.1 us
  transfers between devices with their start and end apart: 8, of which 3 were waited for; matrix products, arithmetic and copies ran while one was open for 49% of the time, Pallas kernels for 0%

commit v1 on v0

v1 whole, which is shorter than its diff:
```python
import functools
import math

import jax
import jax.numpy as jnp
from jax import lax
from jax.experimental import pallas as pl
from jax.experimental.pallas import tpu as pltpu
from jax.sharding import PartitionSpec as P

D = 768
HEADS = 12
HEAD = 64
FF = 3072
DEC = 512
PATCHES = 196
KEEP = 49
IMG = 32
HALF = 16
ROWS = IMG * KEEP
HROWS = HALF * KEEP
PADK = 64
UNITS = 3
EPSILON = 1e-06
BF = jnp.bfloat16
F32 = jnp.float32
MIB = 1 << 20

NN = (((1,), (0,)), ((), ()))
NT = (((1,), (1,)), ((), ()))
TN = (((0,), (0,)), ((), ()))


def dot(left, right, dims=NN):
    return lax.dot_general(left, right, dims, preferred_element_type=F32)


def params(mib=60):
    return pltpu.CompilerParams(vmem_limit_bytes=mib * MIB)


def whole(shape):
    return pl.BlockSpec(shape, lambda *_: (0,) * len(shape), pipeline_mode=pl.Buffered(1))


def norm(values):
    centered = values - jnp.mean(values, axis=-1, keepdims=True)
    inv = lax.rsqrt(jnp.mean(centered * centered, axis=-1, keepdims=True) + EPSILON)
    return centered * inv, inv


def norm_back(unit, inv, grad, gain):
    f = grad * gain
    return inv * (
        f
        - jnp.mean(f, axis=-1, keepdims=True)
        - unit * jnp.mean(f * unit, axis=-1, keepdims=True)
    )


def col_sum(values):
    return jnp.sum(values, axis=0, keepdims=True)


def gelu_pair(v):
    z = jnp.abs(v) * (1 / math.sqrt(2.0))
    t = 1.0 / (1.0 + 0.3275911 * z)
    e = jnp.exp(-z * z)
    poly = t * (
        0.5 * 0.254829592
        + t
        * (
            0.5 * -0.284496736
            + t * (0.5 * 1.421413741 + t * (0.5 * -1.453152027 + t * (0.5 * 1.061405429)))
        )
    )
    tail = poly * e
    cdf = jnp.where(v >= 0, 1.0 - tail, tail)
    return v * cdf, cdf + v * (e * (1 / math.sqrt(2 * math.pi)))


def one_hot(rows, code):
    at = lax.broadcasted_iota(jnp.int32, (rows, code.shape[1]), 0)
    return jnp.where(at == code, 1.0, 0.0).astype(BF)


def owner_blocks(seq_count):
    dev_blocks = PATCHES
    most = -(-dev_blocks // seq_count)
    return dev_blocks, most, -(-most // 4) * 4


def first_block(seq_count, t):
    return lax.rem(
        t + seq_count - lax.rem(lax.axis_index("seq") * PATCHES, seq_count), seq_count
    )


def pick_kernel(seq_count, slots, code_ref, dec_ref, out_ref, sum_ref):
    t = pl.program_id(0)
    dev_blocks, most, padded = owner_blocks(seq_count)
    start = first_block(seq_count, t)
    pieces = []
    for m in range(most):
        at = start + m * seq_count
        clamped = jnp.minimum(at, dev_blocks - 1)
        pieces.append(dec_ref[pl.ds(pl.multiple_of(clamped * IMG, IMG), IMG), :])
    if padded > most:
        pieces.append(jnp.zeros(((padded - most) * IMG, DEC), BF))
    picked = dot(one_hot(slots * IMG + 16, code_ref[0]), jnp.concatenate(pieces, axis=0))
    out_ref[...] = picked[: slots * IMG].astype(BF).reshape(slots, IMG, DEC)

    @pl.when(t == 0)
    def _():
        sum_ref[...] = jnp.zeros_like(sum_ref)

    sum_ref[...] += picked[slots * IMG : slots * IMG + 8]


def pick(seq_count, slots, code, dec_grad):
    return pl.pallas_call(
        functools.partial(pick_kernel, seq_count, slots),
        grid=(seq_count,),
        in_specs=[
            pl.BlockSpec((1, 1, code.shape[2]), lambda t: (t, 0, 0)),
            whole(dec_grad.shape),
        ],
        out_specs=[
            pl.BlockSpec((slots, IMG, DEC), lambda t: (t, 0, 0)),
            pl.BlockSpec((8, DEC), lambda t: (0, 0)),
        ],
        out_shape=[
            jax.ShapeDtypeStruct((seq_count * slots, IMG, DEC), BF),
            jax.ShapeDtypeStruct((8, DEC), F32),
        ],
        compiler_params=params(),
        name="pick",
    )(code, dec_grad)


def place_kernel(seq_count, slots, code_ref, arrived_ref, mask_ref, out_ref):
    t = pl.program_id(0)
    dev_blocks, most, padded = owner_blocks(seq_count)
    start = first_block(seq_count, t)
    fill = jnp.where(
        lax.broadcasted_iota(jnp.int32, (16, DEC), 0) == 0, mask_ref[...], 0.0
    ).astype(BF)
    source = jnp.concatenate([arrived_ref[...].reshape(slots * IMG, DEC), fill], axis=0)
    spread = dot(one_hot(slots * IMG + 16, code_ref[0]), source, TN).astype(BF)
    for m in range(most):
        at = start + m * seq_count
        piece = spread[m * IMG : (m + 1) * IMG]
        if (m + 1) * seq_count <= dev_blocks:
            out_ref[pl.ds(pl.multiple_of(at * IMG, IMG), IMG), :] = piece
        else:

            @pl.when(at < dev_blocks)
            def _():
                out_ref[pl.ds(pl.multiple_of(at * IMG, IMG), IMG), :] = piece


def place(seq_count, slots, code, arrived, mask_token):
    return pl.pallas_call(
        functools.partial(place_kernel, seq_count, slots),
        grid=(seq_count,),
        in_specs=[
            pl.BlockSpec((1, 1, code.shape[2]), lambda t: (t, 0, 0)),
            pl.BlockSpec((slots, IMG, DEC), lambda t: (t, 0, 0)),
            whole((1, DEC)),
        ],
        out_specs=whole((PATCHES * IMG, DEC)),
        out_shape=jax.ShapeDtypeStruct((PATCHES * IMG, DEC), BF),
        compiler_params=params(),
        name="place",
    )(code, arrived, mask_token)


def pack_kernel(code_ref, rows_ref, out_ref):
    count = out_ref.shape[0]
    picked = dot(one_hot(count * HALF, code_ref[0]), rows_ref[...])
    out_ref[...] = picked.astype(BF).reshape(count, HALF, DEC)


def pack(code, rows, count):
    return pl.pallas_call(
        pack_kernel,
        grid=(2,),
        in_specs=[
            pl.BlockSpec((1, 1, HROWS), lambda g: (g, 0, 0)),
            pl.BlockSpec((HROWS, DEC), lambda g: (g, 0)),
        ],
        out_specs=pl.BlockSpec((count, HALF, DEC), lambda g: (0, g, 0)),
        out_shape=jax.ShapeDtypeStruct((count, IMG, DEC), BF),
        compiler_params=params(),
        name="pack",
    )(code, rows)


def unpack_kernel(code_ref, slots_ref, out_ref):
    count = slots_ref.shape[0]
    source = slots_ref[...].reshape(count * HALF, DEC)
    out_ref[...] = dot(one_hot(count * HALF, code_ref[0]), source, TN).astype(BF)


def unpack(code, slots):
    count = slots.shape[0]
    return pl.pallas_call(
        unpack_kernel,
        grid=(2,),
        in_specs=[
            pl.BlockSpec((1, 1, HROWS), lambda g: (g, 0, 0)),
            pl.BlockSpec((count, HALF, DEC), lambda g: (0, g, 0)),
        ],
        out_specs=pl.BlockSpec((HROWS, DEC), lambda g: (g, 0)),
        out_shape=jax.ShapeDtypeStruct((ROWS, DEC), BF),
        compiler_params=params(),
        name="unpack",
    )(code, slots)


UNIT = 4 * HEAD


def block_diag(rows):
    lane_head = lax.broadcasted_iota(jnp.int32, rows.shape, 1) // HEAD
    zero = jnp.zeros_like(rows)
    return jnp.concatenate([jnp.where(lane_head == h, rows, zero) for h in range(4)], axis=0)


def fold_heads(left, right):
    low = lax.broadcasted_iota(jnp.int32, (PADK, 2 * HEAD), 1) < HEAD
    return jnp.concatenate(
        [
            jnp.where(low, left[:PADK], left[PADK:]),
            jnp.where(low, right[:PADK], right[PADK:]),
        ],
        axis=1,
    )


def soft_cols(key, query_diag):
    scores = dot(key, query_diag, NT)
    valid = lax.broadcasted_iota(jnp.int32, scores.shape, 0) < KEEP
    scores = jnp.where(valid, scores, -1e30)
    e = jnp.exp(scores - jnp.max(scores, axis=0, keepdims=True))
    return e * (1.0 / jnp.sum(e, axis=0, keepdims=True))


def each_image(image, *refs):
    def group(g, carry):
        base = pl.multiple_of(g * 8 * KEEP, 8)
        views = [ref.at[pl.ds(base, 8 * KEEP + 16)] for ref in refs]
        for near in range(8):
            image(g * 8 + near, near, *views)
        return carry

    lax.fori_loop(0, HALF // 8, group, 0)


def attn_fwd_kernel(
    x_ref, gain_ref, shift_ref, wqkv_ref, bias_ref, wout_ref, obias_ref,
    qkvp_ref, att_ref, hidden_ref, qs, ats,
):
    x = x_ref[...].astype(F32)
    unit, _ = norm(x)
    first = (unit * gain_ref[...] + shift_ref[...]).astype(BF)
    for c in range(3):
        cols = slice(c * D, (c + 1) * D)
        qs[:HROWS, cols] = (
            (dot(first, wqkv_ref[:, cols]) + bias_ref[:, cols]).astype(BF).astype(F32)
        )
    qs[HROWS:, :] = jnp.zeros((16, 3 * D), F32)

    def image(i, near, qs, ats):
        r0 = near * KEEP
        for u in range(UNITS):
            part = []
            for c in range(3):
                cols = slice(c * D + u * UNIT, c * D + (u + 1) * UNIT)
                rows = qs[r0 : r0 + PADK, cols].astype(BF)
                qkvp_ref[i, :, cols] = rows
                part.append(rows)
            q, k, v = part
            probs = soft_cols(k, block_diag(q * BF(0.125))).astype(BF)
            out = fold_heads(
                dot(probs[:, :128], v[:, :128], TN), dot(probs[:, 128:], v[:, 128:], TN)
            )
            ats[r0 : r0 + 56, u * UNIT : (u + 1) * UNIT] = out[:56]

    each_image(image, qs, ats)
    att = ats[:HROWS, :].astype(BF)
    att_ref[...] = att
    hidden_ref[...] = x_ref[...].astype(F32) + (dot(att, wout_ref[...]) + obias_ref[...])


def attn_fwd(x, gain, shift, wqkv, bias, wout, obias):
    return pl.pallas_call(
        attn_fwd_kernel,
        grid=(2,),
        in_specs=[
            pl.BlockSpec((HROWS, D), lambda g: (g, 0)),
            whole((1, D)),
            whole((1, D)),
            whole((D, 3 * D)),
            whole((1, 3 * D)),
            whole((D, D)),
            whole((1, D)),
        ],
        out_specs=[
            pl.BlockSpec((HALF, PADK, 3 * D), lambda g: (g, 0, 0)),
            pl.BlockSpec((HROWS, D), lambda g: (g, 0)),
            pl.BlockSpec((HROWS, D), lambda g: (g, 0)),
        ],
        out_shape=[
            jax.ShapeDtypeStruct((IMG, PADK, 3 * D), BF),
            jax.ShapeDtypeStruct((ROWS, D), BF),
            jax.ShapeDtypeStruct((ROWS, D), F32),
        ],
        scratch_shapes=[pltpu.VMEM((HROWS + 16, 3 * D), F32), pltpu.VMEM((HROWS + 16, D), F32)],
        compiler_params=params(),
        name="attn_fwd",
    )(x, gain, shift, wqkv, bias, wout, obias)


def attn_bwd_kernel(
    hgrad_ref, att_ref, qkvp_ref, x_ref, gain_ref, shift_ref, wout_ref, wqkv_ref,
    pgrad_ref, wqkvg_ref, woutg_ref, obias_ref, qkvb_ref, lng_ref, lns_ref,
    ags, dqs, wqacc, woacc,
):
    g = pl.program_id(0)

    @pl.when(g == 0)
    def _():
        wqacc[...] = jnp.zeros_like(wqacc)
        woacc[...] = jnp.zeros_like(woacc)
        for ref in (obias_ref, qkvb_ref, lng_ref, lns_ref):
            ref[...] = jnp.zeros_like(ref)

    branch = hgrad_ref[...].astype(BF)
    obias_ref[...] += col_sum(branch.astype(F32))
    woacc[...] += dot(att_ref[...], branch, TN)
    ags[:HROWS, :] = dot(branch, wout_ref[...], NT)
    ags[HROWS:, :] = jnp.zeros((16, D), F32)

    def image(i, near, ags, dqs):
        r0 = near * KEEP
        valid = lax.broadcasted_iota(jnp.int32, (PADK, UNIT), 0) < KEEP
        for u in range(UNITS):
            q, k, v = (
                qkvp_ref[i, :, c * D + u * UNIT : c * D + (u + 1) * UNIT] for c in range(3)
            )
            q_diag = block_diag(q * BF(0.125))
            probs = soft_cols(k, q_diag)
            probs_in = probs.astype(BF)
            agrad = jnp.where(
                valid, ags[r0 : r0 + PADK, u * UNIT : (u + 1) * UNIT], 0.0
            ).astype(BF)
            a_diag = block_diag(agrad)
            pgrad = dot(v, a_diag, NT)
            vgrad = dot(probs_in, a_diag)
            inner = jnp.sum(probs * pgrad, axis=0, keepdims=True)
            sgrad = (probs * (pgrad - inner)).astype(BF)
            kgrad = dot(sgrad, q_diag)
            qgrad = 0.125 * fold_heads(
                dot(sgrad[:, :128], k[:, :128], TN), dot(sgrad[:, 128:], k[:, 128:], TN)
            )
            for c, grad in enumerate((qgrad, kgrad, vgrad)):
                dqs[r0 : r0 + 56, c * D + u * UNIT : c * D + (u + 1) * UNIT] = grad[:56]

    each_image(image, ags, dqs)
    unit, inv = norm(x_ref[...].astype(F32))
    first = (unit * gain_ref[...] + shift_ref[...]).astype(BF)
    fgrad = None
    for c in range(3):
        cols = slice(c * D, (c + 1) * D)
        grad = dqs[:HROWS, cols].astype(BF)
        qkvb_ref[:, cols] += col_sum(grad.astype(F32))
        wqacc[:, cols] += dot(first, grad, TN)
        term = dot(grad, wqkv_ref[:, cols], NT)
        fgrad = term if fgrad is None else fgrad + term
    lng_ref[...] += col_sum(fgrad * unit)
    lns_ref[...] += col_sum(fgrad)
    pgrad_ref[...] = (hgrad_ref[...] + norm_back(unit, inv, fgrad, gain_ref[...])).astype(BF)

    @pl.when(g == 1)
    def _():
        wqkvg_ref[...] = wqacc[...].astype(BF)
        woutg_ref[...] = woacc[...].astype(BF)


def attn_bwd(hgrad, att, qkvp, x, gain, shift, wout, wqkv):
    rows = pl.BlockSpec((HROWS, D), lambda g: (g, 0))
    return pl.pallas_call(
        attn_bwd_kernel,
        grid=(2,),
        in_specs=[
            rows,
            rows,
            pl.BlockSpec((HALF, PADK, 3 * D), lambda g: (g, 0, 0)),
            rows,
            whole((1, D)),
            whole((1, D)),
            whole((D, D)),
            whole((D, 3 * D)),
        ],
        out_specs=[
            rows,
            whole((D, 3 * D)),
            whole((D, D)),
            whole((1, D)),
            whole((1, 3 * D)),
            whole((1, D)),
            whole((1, D)),
        ],
        out_shape=[
            jax.ShapeDtypeStruct((ROWS, D), BF),
            jax.ShapeDtypeStruct((D, 3 * D), BF),
            jax.ShapeDtypeStruct((D, D), BF),
            jax.ShapeDtypeStruct((1, D), F32),
            jax.ShapeDtypeStruct((1, 3 * D), F32),
            jax.ShapeDtypeStruct((1, D), F32),
            jax.ShapeDtypeStruct((1, D), F32),
        ],
        scratch_shapes=[
            pltpu.VMEM((HROWS + 16, D), F32),
            pltpu.VMEM((HROWS + 16, 3 * D), F32),
            pltpu.VMEM((D, 3 * D), F32),
            pltpu.VMEM((D, D), F32),
        ],
        compiler_params=params(),
        name="attn_bwd",
    )(hgrad, att, qkvp, x, gain, shift, wout, wqkv)


FTILE = 512
FSTEPS = FF // FTILE


def mlp_fwd_kernel(
    hidden_ref, gain_ref, shift_ref, w1_ref, b1_ref, w2_ref, b2_ref, we_ref, be_ref,
    act_ref, slope_ref, block_ref, emb_ref, second, acc,
):
    f = pl.program_id(0)

    @pl.when(f == 0)
    def _():
        unit, _ = norm(hidden_ref[...])
        second[...] = (unit * gain_ref[...] + shift_ref[...]).astype(BF)
        acc[...] = hidden_ref[...] + b2_ref[...]

    for h in range(2):
        rows = slice(h * HROWS, (h + 1) * HROWS)
        active, slope = gelu_pair(dot(second[rows, :], w1_ref[...]) + b1_ref[...])
        active = active.astype(BF)
        act_ref[rows, :] = active
        slope_ref[rows, :] = slope.astype(BF)
        acc[rows, :] += dot(active, w2_ref[...])

    @pl.when(f == FSTEPS - 1)
    def _():
        block_in = acc[...].astype(BF)
        block_ref[...] = block_in
        emb_ref[...] = (dot(block_in, we_ref[...]) + be_ref[...]).astype(BF)


def mlp_fwd(hidden, gain, shift, w1, b1, w2, b2, we, be):
    tile = pl.BlockSpec((ROWS, FTILE), lambda f: (0, f))
    return pl.pallas_call(
        mlp_fwd_kernel,
        grid=(FSTEPS,),
        in_specs=[
            whole((ROWS, D)),
            whole((1, D)),
            whole((1, D)),
            pl.BlockSpec((D, FTILE), lambda f: (0, f)),
            pl.BlockSpec((1, FTILE), lambda f: (0, f)),
            pl.BlockSpec((FTILE, D), lambda f: (f, 0)),
            whole((1, D)),
            whole((D, DEC)),
            whole((1, DEC)),
        ],
        out_specs=[tile, tile, whole((ROWS, D)), whole((ROWS, DEC))],
        out_shape=[
            jax.ShapeDtypeStruct((ROWS, FF), BF),
            jax.ShapeDtypeStruct((ROWS, FF), BF),
            jax.ShapeDtypeStruct((ROWS, D), BF),
            jax.ShapeDtypeStruct((ROWS, DEC), BF),
        ],
        scratch_shapes=[pltpu.VMEM((ROWS, D), BF), pltpu.VMEM((ROWS, D), F32)],
        compiler_params=params(),
        name="mlp_fwd",
    )(hidden, gain, shift, w1, b1, w2, b2, we, be)


def mlp_bwd_kernel(
    egrad_ref, block_ref, hidden_ref, gain_ref, shift_ref, we_ref, act_ref, slope_ref, w2_ref, w1_ref,
    hgrad_ref, weg_ref, ebias_ref, w2g_ref, b2_ref, w1g_ref, b1_ref, lng_ref, lns_ref,
    two, second, acc,
):
    f = pl.program_id(0)

    @pl.when(f == 0)
    def _():
        egrad = egrad_ref[...]
        weg_ref[...] = dot(block_ref[...], egrad, TN).astype(BF)
        ebias_ref[...] = col_sum(egrad.astype(F32))
        out_grad = dot(egrad, we_ref[...], NT)
        hgrad_ref[...] = out_grad
        two_grad = out_grad.astype(BF)
        two[...] = two_grad
        b2_ref[...] = col_sum(two_grad.astype(F32))
        unit, _ = norm(hidden_ref[...])
        second[...] = (unit * gain_ref[...] + shift_ref[...]).astype(BF)
        acc[...] = jnp.zeros_like(acc)

    w2g_ref[...] = dot(act_ref[...], two[...], TN).astype(BF)
    inner = (dot(two[...], w2_ref[...], NT) * slope_ref[...].astype(F32)).astype(BF)
    b1_ref[...] = col_sum(inner.astype(F32))
    w1g_ref[...] = dot(second[...], inner, TN).astype(BF)
    acc[...] += dot(inner, w1_ref[...], NT)

    @pl.when(f == FSTEPS - 1)
    def _():
        unit, inv = norm(hidden_ref[...])
        grad = acc[...]
        lng_ref[...] = col_sum(grad * unit)
        lns_ref[...] = col_sum(grad)
        hgrad_ref[...] += norm_back(unit, inv, grad, gain_ref[...])


def mlp_bwd(egrad, block_in, hidden, gain, shift, we, act, slope, w2, w1):
    tile = pl.BlockSpec((ROWS, FTILE), lambda f: (0, f))
    return pl.pallas_call(
        mlp_bwd_kernel,
        grid=(FSTEPS,),
        in_specs=[
            whole((ROWS, DEC)),
            whole((ROWS, D)),
            whole((ROWS, D)),
            whole((1, D)),
            whole((1, D)),
            whole((D, DEC)),
            tile,
            tile,
            pl.BlockSpec((FTILE, D), lambda f: (f, 0)),
            pl.BlockSpec((D, FTILE), lambda f: (0, f)),
        ],
        out_specs=[
            whole((ROWS, D)),
            whole((D, DEC)),
            whole((1, DEC)),
            pl.BlockSpec((FTILE, D), lambda f: (f, 0)),
            whole((1, D)),
            pl.BlockSpec((D, FTILE), lambda f: (0, f)),
            pl.BlockSpec((1, FTILE), lambda f: (0, f)),
            whole((1, D)),
            whole((1, D)),
        ],
        out_shape=[
            jax.ShapeDtypeStruct((ROWS, D), F32),
            jax.ShapeDtypeStruct((D, DEC), BF),
            jax.ShapeDtypeStruct((1, DEC), F32),
            jax.ShapeDtypeStruct((FF, D), BF),
            jax.ShapeDtypeStruct((1, D), F32),
            jax.ShapeDtypeStruct((D, FF), BF),
            jax.ShapeDtypeStruct((1, FF), F32),
            jax.ShapeDtypeStruct((1, D), F32),
            jax.ShapeDtypeStruct((1, D), F32),
        ],
        scratch_shapes=[
            pltpu.VMEM((ROWS, D), BF),
            pltpu.VMEM((ROWS, D), BF),
            pltpu.VMEM((ROWS, D), F32),
        ],
        compiler_params=params(),
        name="mlp_bwd",
    )(egrad, block_in, hidden, gain, shift, we, act, slope, w2, w1)


def decoder_codes(keep_index, slots):
    seq_count = lax.axis_size("seq")
    dev_blocks, _, padded = owner_blocks(seq_count)
    t = jnp.arange(seq_count, dtype=jnp.int32)
    start = first_block(seq_count, t)
    lowest = (lax.axis_index("seq") * PATCHES + start) // seq_count
    m = jnp.arange(padded, dtype=jnp.int32)
    valid = (start[:, None] + m[None, :] * seq_count) < dev_blocks
    place_at = (lowest[:, None] + m[None, :])[None, :, :, None]
    kept = keep_index.T.reshape(KEEP, seq_count, 1, IMG)
    hit = jnp.sum((kept == place_at).astype(jnp.int32), axis=0)
    below = (kept < place_at) & (kept >= lowest[None, :, None, None])
    rank = jnp.sum(below.astype(jnp.int32), axis=0)
    image = jnp.arange(IMG, dtype=jnp.int32)
    code = jnp.where(hit > 0, rank * IMG + image, slots * IMG)
    code = jnp.where(valid[:, :, None], code, -1)
    return code.reshape(seq_count, 1, padded * IMG)


def image_codes(keep_index, slots):
    seq_count = lax.axis_size("seq")
    group_imgs = keep_index.shape[0]
    at = lax.axis_index("seq") * IMG
    own = lax.dynamic_slice_in_dim(keep_index, at, IMG, 0)
    image = jnp.arange(IMG, dtype=jnp.int32)[:, None]
    owner = (own * group_imgs + at + image) // (IMG * PATCHES)
    lower = jnp.sum((owner[:, None, :] < owner[:, :, None]).astype(jnp.int32), axis=2)
    rank = jnp.arange(KEEP, dtype=jnp.int32)[None, :] - lower
    code = (owner * slots + rank) * HALF + image % HALF
    return code.reshape(2, 1, HROWS)


def local(
    patches,
    keep_index,
    ln1_gain,
    ln1_shift,
    w_qkv,
    q_bias,
    v_bias,
    w_out,
    out_bias,
    ln2_gain,
    ln2_shift,
    w_fc1,
    fc1_bias,
    w_fc2,
    fc2_bias,
    w_embed,
    embed_bias,
    mask_token,
    decoder_grad,
):
    seq_count = lax.axis_size("seq")
    slots = 2 * KEEP // seq_count
    row = lambda v: v.reshape(1, -1)
    dec_code = decoder_codes(keep_index, slots)
    img_code = image_codes(keep_index, slots)
    grad_slots, mask_rows = pick(seq_count, slots, dec_code, decoder_grad)
    returned = lax.all_to_all(grad_slots, "seq", split_axis=0, concat_axis=0, tiled=True)

    qkv_bias = jnp.concatenate([q_bias, jnp.zeros_like(q_bias), v_bias])
    qkvp, attended, hidden = attn_fwd(
        patches, row(ln1_gain), row(ln1_shift), w_qkv, row(qkv_bias), w_out, row(out_bias)
    )
    active, slope, block_in, embedded = mlp_fwd(
        hidden, row(ln2_gain), row(ln2_shift), w_fc1, row(fc1_bias), w_fc2, row(fc2_bias),
        w_embed, row(embed_bias),
    )
    send = pack(img_code, embedded, seq_count * slots)
    arrived = lax.all_to_all(send, "seq", split_axis=0, concat_axis=0, tiled=True)

    embed_grad = unpack(img_code, returned)
    hgrad, weg, ebias, w2g, b2, w1g, b1, ln2g, ln2s = mlp_bwd(
        embed_grad, block_in, hidden, row(ln2_gain), row(ln2_shift), w_embed, active, slope,
        w_fc2, w_fc1,
    )
    patches_grad, wqkvg, woutg, obias, qkvb, ln1g, ln1s = attn_bwd(
        hgrad, attended, qkvp, patches, row(ln1_gain), row(ln1_shift), w_out, w_qkv
    )
    decoder_input = place(seq_count, slots, dec_code, arrived, row(mask_token))

    shares = [
        lax.psum(lax.psum_scatter(v, "seq", scatter_dimension=0, tiled=True), "dp").astype(F32)
        for v in (weg, w2g, w1g, woutg, wqkvg)
    ]
    vectors = [
        ln1g, ln1s, qkvb[:, :D], qkvb[:, 2 * D :], obias, ln2g, ln2s, b1, b2, ebias, mask_rows[:1],
    ]
    packed = jnp.concatenate([v.reshape(seq_count, -1) for v in vectors], axis=1).astype(BF)
    small = lax.psum(
        lax.psum_scatter(packed, "seq", scatter_dimension=0, tiled=True), "dp"
    ).astype(F32).reshape(-1)
    parts, at = [], 0
    for v in vectors:
        size = v.shape[1] // seq_count
        parts.append(small[at : at + size])
        at += size
    ln1g, ln1s, qb, vb, obias, ln2g, ln2s, b1, b2, ebias, mask_grad = parts
    weg, w2g, w1g, woutg, wqkvg = shares
    return (
        decoder_input,
        patches_grad,
        ln1g,
        ln1s,
        wqkvg,
        qb,
        vb,
        woutg,
        obias,
        ln2g,
        ln2s,
        w1g,
        b1,
        w2g,
        b2,
        weg,
        ebias,
        mask_grad,
    )


def solution(mesh):
    rows = P(("dp", "seq"), None)
    placed = (rows, P("dp", None)) + (P(),) * 16 + (rows,)
    vec, mat = P("seq"), P("seq", None)
    return jax.shard_map(
        local,
        mesh=mesh,
        in_specs=placed,
        out_specs=(
            rows, rows, vec, vec, mat, vec, vec, mat, vec, vec, vec, mat, vec, mat, vec, mat, vec, vec,
        ),
        check_vma=False,
    )
```

time: 925 us -> 710 us (0.77)
  matrix products: 267 us -> 0 us
  local copies, waits for them, and re-layouts: 254 us -> 14.7 us
  Pallas kernels: 0 us -> 228 us
  waiting for transfers between devices: 167 us -> 374 us
  other arithmetic: 117 us -> 17.4 us
  blocking collectives: 76.2 us -> 42.4 us
    dot_general x21 -> x0, matrix products: 267 us -> none  [the longest x1 54.5 us: local(): jnp.dot(second_in, w_fc1, preferred_element_type=jnp.float32) + fc1_bias]
    reduce_scatter x5, waiting for transfers between devices: 124 us -> 373 us  [local(): lax.psum_scatter(v, 'seq', scatter_dimension=0, tiled=True)]
    pallas_call x0 -> x8, Pallas kernels: none -> 228 us  [the longest x1 62.9 us: attn_bwd(): pl.pallas_call(attn_bwd_kernel, grid=(2,), in_specs=[rows, rows, pl.Block...]
    gather x6 -> x0, local copies, waits for them, and re-layouts: 75.3 us -> none  [the longest x2 23.1 us: local(): decoder_grad[pick_row]]
    convert_element_type x6 -> x0, local copies, waits for them, and re-layouts: 51.5 us -> none  [the longest x2 33.5 us: local(): qkv_grad = jnp.stack([query_grad, key_grad, value_grad], axis=2).reshape(...]
    psum x1, waiting for transfers between devices: 42.4 us -> 0.01 us  [local(): lax.psum(lax.psum_scatter(v, 'seq', scatter_dimension=0, tiled=True), 'dp')]
    reshape x6 -> x19, local copies, waits for them, and re-layouts: 45.6 us -> 5.69 us  [the longest x7 4.13 us: local(): row = lambda v: v.reshape(1, -1)]
    convert_element_type x19 -> x6, other arithmetic: 41.4 us -> 6.8 us  [the longest x5 6.79 us: local(): lax.psum(lax.psum_scatter(v, 'seq', scatter_dimension=0, tiled=True), 'dp')]
  transfers between devices with their start and end apart: 8 -> 8, of which waited for: 3 -> 4; matrix products, arithmetic and copies ran while one was open for 49% -> 2% of each run, Pallas kernels for 0% -> 23%
where the time goes in v1:
time: 710 us; the launch traced here: 705 us
  waiting for transfers between devices  374 us (53%)
  Pallas kernels  228 us (32%)
  blocking collectives  42.4 us (6%)
  other arithmetic  17.4 us (2%)
  between operations  14.8 us (2%)
  local copies, waits for them, and re-layouts  14.7 us (2%)
  starting transfers between devices  13.9 us (2%)
    reduce_scatter x5, waiting for transfers between devices, local(): lax.psum_scatter(v, 'seq', scatter_dimension=0, tiled=True)  373 us
    pallas_call x1, Pallas kernels, attn_bwd(): pl.pallas_call(attn_bwd_kernel, grid=(2,), in_specs=[rows, rows, pl.Block...  62.9 us
    pallas_call x1, Pallas kernels, mlp_bwd(): pl.pallas_call(mlp_bwd_kernel, grid=(FSTEPS,), in_specs=[whole((ROWS, DEC...  50.4 us
    pallas_call x1, Pallas kernels, attn_fwd(): pl.pallas_call(attn_fwd_kernel, grid=(2,), in_specs=[pl.BlockSpec((HROWS,...  44 us
    pallas_call x1, Pallas kernels, mlp_fwd(): pl.pallas_call(mlp_fwd_kernel, grid=(FSTEPS,), in_specs=[whole((ROWS, D))...  39.6 us
    unnamed x1, blocking collectives  35.9 us
  transfers between devices with their start and end apart: 8, of which 4 were waited for; matrix products, arithmetic and copies ran while one was open for 2% of the time, Pallas kernels for 23%

profile of v1, /device:TPU:0, one launch (start us, length us, event | category | flops | bytes accessed | tf_op | source)
XLA Modules:
  0.0 705.1 jit_solution(13119906005992331570)
XLA Ops:
  7.2 0.9 copy.58
  8.3 8.0 %convert_reduce_fusion = (s32[8,28,32]{2,1,0:T(8,128)S(1)}, s32[8,28,32]{2,1,0:T(8,128)S(1)}) fusion(s32[8,28]{1,0:T(8,128)S(1)} %iota_add_fusion.1, s32[49,8,32]{0,2,1:T(8,128)S(1)} %bitcast.28, pred[49,8,32]{0,2,1:T(8,128)(4,1)S(1)} %broadcast_compare_fusion), kind=kLoop, calls=%fused_computation | loop fusion | flops 2444288 | bytes 120960 | tf_op jit(solution)/shard_map/reduce_sum | solution.py:592
  16.4 0.1 mul.61
  16.5 0.1 gt.19
  16.8 0.1 broadcast_in_dim.38
  17.0 0.7 select_select_fusion.code_ref
  17.7 9.0 %pick.1 = (bf16[96,32,512]{2,1,0:T(8,128)(2,1)}, f32[8,512]{1,0:T(8,128)}) custom-call(s32[8,1,896]{2,1,0:T(1,128)} %select_select_fusion.code_ref, bf16[6272,512]{1,0:T(8,128)(2,1)} %dec_ref.1), custom_call_target="tpu_custom_call" | custom-call | tf_op jit(solution)/shard_map/pick/pallas_call | solution.py:121
  26.8 7.4 %all-to-all-start.1 = ((bf16[96,32,512]{2,1,0:T(8,128)(2,1)}), bf16[96,32,512]{2,1,0:T(8,128)(2,1)S(1)}, u32[]{:S(2)}, u32[]{:S(2)}) async-start(bf16[96,32,512]{2,1,0:T(8,128)(2,1)} %get-tuple-element.45), calls=%async_computation.1 | async-start | bytes 6291456 | tf_op jit(solution)/shard_map/all_to_all | solution.py:639
  34.2 0.3 reduce-scatter.14.cloned.1.call-start
  34.8 1.1 convert_reduce_fusion.2
  36.1 0.7 reshape.333.code_ref
  36.8 0.6 reshape.334.gain_ref
  37.4 0.6 reshape.335.shift_ref
  38.0 0.6 reshape.336.bias_ref
  38.6 0.6 reshape.337.obias_ref
  39.2 0.6 reshape.338.gain_ref
  39.8 0.6 reshape.339.shift_ref
  40.4 0.6 reshape.341.b2_ref
  41.0 44.0 %attn_fwd.1 = (bf16[32,64,2304]{2,1,0:T(8,128)(2,1)}, bf16[1568,768]{1,0:T(8,128)(2,1)}, f32[1568,768]{1,0:T(8,128)}) custom-call(bf16[1568,768]{1,0:T(8,128)(2,1)} %x_ref.3, f32[1,768]{1,0:T(1,128)} %reshape.334.gain_ref, f32[1,768]{1,0:T(1,128)} %reshape.335.shift_ref, bf16[768,2304]{1,0:T(8,128)(2,1)} %wqkv_ref.3, f32[1,2304]{1,0:T(1,128)} %reshape.336.bias_ref, ...), custom_call_target="tpu_custom_call" | custom-call | tf_op jit(solution)/shard_map/attn_fwd/pallas_call | solution.py:297
  85.0 39.6 %mlp_fwd.1 = (bf16[1568,3072]{1,0:T(8,128)(2,1)}, bf16[1568,3072]{1,0:T(8,128)(2,1)}, bf16[1568,768]{1,0:T(8,128)(2,1)}, bf16[1568,512]{1,0:T(8,128)(2,1)}) custom-call(f32[1568,768]{1,0:T(8,128)} %get-tuple-element.43.hidden_ref, f32[1,768]{1,0:T(1,128)} %reshape.338.gain_ref, f32[1,768]{1,0:T(1,128)} %reshape.339.shift_ref, bf16[768,3072]{1,0:T(8,128)(2,1)} %w1_ref.3, ...), custom_call_target="tpu_custom_call" | custom-call | tf_op jit(solution)/shard_map/mlp_fwd/pallas_call | solution.py:468
  124.6 1.7 copy-done
  126.4 5.2 unpack.1.egrad_ref
  131.6 50.4 %mlp_bwd.1 = (f32[1568,768]{1,0:T(8,128)}, bf16[768,512]{1,0:T(8,128)(2,1)}, f32[1,512]{1,0:T(1,128)}, bf16[3072,768]{1,0:T(8,128)(2,1)}, f32[1,768]{1,0:T(1,128...) custom-call(bf16[1568,512]{1,0:T(8,128)(2,1)} %unpack.1.egrad_ref, ...), custom_call_target="tpu_custom_call" | custom-call | tf_op jit(solution)/shard_map/mlp_bwd/pallas_call | solution.py:533
  182.1 62.9 %attn_bwd.1 = (bf16[1568,768]{1,0:T(8,128)(2,1)}, bf16[768,2304]{1,0:T(8,128)(2,1)}, bf16[768,768]{1,0:T(8,128)(2,1)}, f32[1,768]{1,0:T(1,128)}, f32[1,2304]{1,0...) custom-call(f32[1568,768]{1,0:T(8,128)} %get-tuple-element.49.hgrad_ref, bf16[1568,768]{1,0:T(8,128)(2,1)} %get-tuple-element.50.att_ref, ...), custom_call_target="tpu_custom_call" | custom-call | tf_op jit(solution)/shard_map/attn_bwd/pallas_call | solution.py:393
  245.1 0.7 reduce-scatter.6.cloned.1.call-update
  245.8 0.5 reduce-scatter.10.cloned.1.call-update
  246.4 0.5 reduce-scatter.12.cloned.1.call-update
  246.9 6.0 pack.1
  253.0 6.0 all-to-all-start
  259.0 0.7 fusion.1
  259.8 0.6 dynamic-slice
  260.7 91.9 %reduce-scatter.8.cloned.1.call-done = bf16[96,768]{1,0:T(8,128)(2,1)} async-done(((bf16[768,768]{1,0:T(8,128)(2,1)}), bf16[96,768]{1,0:T(8,128)(2,1)}) %reduce-scatter.8.cloned.1.call-update) | async-done | bytes 147472 | tf_op jit(solution)/shard_map/reduce_scatter | solution.py:663
  352.6 82.8 %reduce-scatter.6.cloned.1.call-done = bf16[96,2304]{1,0:T(8,128)(2,1)} async-done(((bf16[768,2304]{1,0:T(8,128)(2,1)}), bf16[96,2304]{1,0:T(8,128)(2,1)}) %reduce-scatter.6.cloned.1.call-update) | async-done | bytes 442384 | tf_op jit(solution)/shard_map/reduce_scatter | solution.py:663
  435.5 98.8 %reduce-scatter.10.cloned.1.call-done = bf16[96,3072]{1,0:T(8,128)(2,1)} async-done(((bf16[768,3072]{1,0:T(8,128)(2,1)}), bf16[96,3072]{1,0:T(8,128)(2,1)}) %reduce-scatter.10.cloned.1.call-update) | async-done | bytes 589840 | tf_op jit(solution)/shard_map/reduce_scatter | solution.py:663
  534.2 99.0 %reduce-scatter.12.cloned.1.call-done = bf16[384,768]{1,0:T(8,128)(2,1)} async-done(((bf16[3072,768]{1,0:T(8,128)(2,1)}), bf16[384,768]{1,0:T(8,128)(2,1)}) %reduce-scatter.12.cloned.1.call-update) | async-done | bytes 589840 | tf_op jit(solution)/shard_map/reduce_scatter | solution.py:663
  634.2 35.9 %all-reduce = bf16[8,1280]{1,0:T(8,128)(2,1)S(1)} all-reduce(bf16[8,1280]{1,0:T(8,128)(2,1)S(1)} %concatenate.8), channel_id=2, replica_groups=mesh['dp'=4,'seq'=8] {'seq'}, use_global_device_ids=true, to_apply=%region_3.4.clone | all-reduce | flops 10240 | bytes 40960
  670.1 0.7 constant_dynamic-slice_fusion
  670.8 6.5 psum.42
  677.3 1.7 copy-done.1
  679.0 10.4 %place.1 = bf16[6272,512]{1,0:T(8,128)(2,1)} custom-call(s32[8,1,896]{2,1,0:T(1,128)} %select_select_fusion.code_ref, bf16[96,32,512]{2,1,0:T(8,128)(2,1)} %copy-done.1, f32[1,512]{1,0:T(1,128)} %bitcast.30), custom_call_target="tpu_custom_call" | custom-call | tf_op jit(solution)/shard_map/place/pallas_call | solution.py:163
  689.3 0.7 slice_reduce_fusion.2
  690.0 0.6 slice_bitcast_fusion
  690.6 0.6 slice_bitcast_fusion.2
  691.2 2.2 convert_element_type.34
  693.4 2.2 convert_element_type.35
  695.6 1.0 convert_element_type.32
  696.6 0.7 convert_element_type.33
  697.3 0.7 convert_element_type.36
  (98 shorter events, 2.4 us)
Async XLA Ops:
  26.7 7.9 %copy-start.3 = (s32[256,49]{0,1:T(8,128)S(1)}, s32[256,49]{0,1:T(8,128)}, u32[]{:S(2)}) copy-start(s32[256,49]{0,1:T(8,128)} %param.20) | copy-start | bytes 150532
  26.7 10.1 %copy-start.8 = (f32[768]{0:T(1024)S(1)}, f32[768]{0:T(1024)}, u32[]{:S(2)}) copy-start(f32[768]{0:T(1024)} %param.21) | copy-start | bytes 9220
  26.7 10.7 %copy-start.9 = (f32[768]{0:T(1024)S(1)}, f32[768]{0:T(1024)}, u32[]{:S(2)}) copy-start(f32[768]{0:T(1024)} %param.22) | copy-start | bytes 9220
  26.7 11.2 %copy-start.14 = (f32[768]{0:T(1024)S(1)}, f32[768]{0:T(1024)}, u32[]{:S(2)}) copy-start(f32[768]{0:T(1024)} %param.25) | copy-start | bytes 9220
  26.7 11.2 %copy-start.15 = (f32[768]{0:T(1024)S(1)}, f32[768]{0:T(1024)}, u32[]{:S(2)}) copy-start(f32[768]{0:T(1024)} %param.24) | copy-start | bytes 9220
  26.7 11.8 %copy-start.10 = (f32[768]{0:T(1024)S(1)}, f32[768]{0:T(1024)}, u32[]{:S(2)}) copy-start(f32[768]{0:T(1024)} %param.27) | copy-start | bytes 9220
  26.8 12.4 %copy-start.11 = (f32[768]{0:T(1024)S(1)}, f32[768]{0:T(1024)}, u32[]{:S(2)}) copy-start(f32[768]{0:T(1024)} %param.28) | copy-start | bytes 9220
  26.8 13.0 %copy-start.12 = (f32[768]{0:T(1024)S(1)}, f32[768]{0:T(1024)}, u32[]{:S(2)}) copy-start(f32[768]{0:T(1024)} %param.29) | copy-start | bytes 9220
  26.8 13.6 %copy-start.13 = (f32[768]{0:T(1024)S(1)}, f32[768]{0:T(1024)}, u32[]{:S(2)}) copy-start(f32[768]{0:T(1024)} %param.33) | copy-start | bytes 9220
  26.8 97.8 %all-to-all-start.1 = ((bf16[96,32,512]{2,1,0:T(8,128)(2,1)}), bf16[96,32,512]{2,1,0:T(8,128)(2,1)S(1)}, u32[]{:S(2)}, u32[]{:S(2)}) async-start(bf16[96,32,512]{2,1,0:T(8,128)(2,1)} %get-tuple-element.45), calls=%async_computation.1 | async-start | bytes 6291456 | tf_op jit(solution)/shard_map/all_to_all | solution.py:639
  34.2 226.5 %reduce-scatter.14.cloned.1.call-start = ((), (), s32[]{:S(2)}) async-start(), calls=%async_computation.11 | async-start | bytes 884736 | tf_op jit(solution)/shard_map/reduce_scatter | solution.py:663
  124.6 1.7 copy-start
  182.0 170.6 %reduce-scatter.8.cloned.1.call-start = ((), (), s32[]{:S(2)}) async-start(), calls=%async_computation.8 | async-start | bytes 1327104 | tf_op jit(solution)/shard_map/reduce_scatter | solution.py:663
  245.0 190.4 %reduce-scatter.6.cloned.1.call-start = ((), (), s32[]{:S(2)}) async-start(), calls=%async_computation.7 | async-start | bytes 3981312 | tf_op jit(solution)/shard_map/reduce_scatter | solution.py:663
  245.8 288.5 %reduce-scatter.10.cloned.1.call-start = ((), (), s32[]{:S(2)}) async-start(), calls=%async_computation.9 | async-start | bytes 5308416 | tf_op jit(solution)/shard_map/reduce_scatter | solution.py:663
  246.3 386.9 %reduce-scatter.12.cloned.1.call-start = ((), (), s32[]{:S(2)}) async-start(), calls=%async_computation.10 | async-start | bytes 5308416 | tf_op jit(solution)/shard_map/reduce_scatter | solution.py:663
  252.9 6.9 copy-start.23
  252.9 7.5 %copy-start.7 = (f32[1,2304]{1,0:T(1,128)S(1)}, f32[1,2304]{1,0:T(1,128)}, u32[]{:S(2)}) copy-start(f32[1,2304]{1,0:T(1,128)} %get-tuple-element.55) | copy-start | bytes 27652
  252.9 7.5 %copy-start.21 = (f32[1,768]{1,0:T(1,128)S(1)}, f32[1,768]{1,0:T(1,128)}, u32[]{:S(2)}) copy-start(f32[1,768]{1,0:T(1,128)} %get-tuple-element.53) | copy-start | bytes 9220
  252.9 7.6 %copy-start.20 = (f32[1,768]{1,0:T(1,128)S(1)}, f32[1,768]{1,0:T(1,128)}, u32[]{:S(2)}) copy-start(f32[1,768]{1,0:T(1,128)} %get-tuple-element.54) | copy-start | bytes 9220
  252.9 7.6 %copy-start.19 = (f32[1,768]{1,0:T(1,128)S(1)}, f32[1,768]{1,0:T(1,128)}, u32[]{:S(2)}) copy-start(f32[1,768]{1,0:T(1,128)} %get-tuple-element.56) | copy-start | bytes 9220
  252.9 7.6 %copy-start.18 = (f32[1,768]{1,0:T(1,128)S(1)}, f32[1,768]{1,0:T(1,128)}, u32[]{:S(2)}) copy-start(f32[1,768]{1,0:T(1,128)} %get-tuple-element.57) | copy-start | bytes 9220
  252.9 7.6 %copy-start.17 = (f32[1,768]{1,0:T(1,128)S(1)}, f32[1,768]{1,0:T(1,128)}, u32[]{:S(2)}) copy-start(f32[1,768]{1,0:T(1,128)} %get-tuple-element.58) | copy-start | bytes 9220
  252.9 7.7 %copy-start.6 = (f32[1,3072]{1,0:T(1,128)S(1)}, f32[1,3072]{1,0:T(1,128)}, u32[]{:S(2)}) copy-start(f32[1,3072]{1,0:T(1,128)} %get-tuple-element.59) | copy-start | bytes 36868
  253.0 380.3 %copy-start.16 = (f32[1,768]{1,0:T(1,128)S(1)}, f32[1,768]{1,0:T(1,128)}, u32[]{:S(2)}) copy-start(f32[1,768]{1,0:T(1,128)} %get-tuple-element.60) | copy-start | bytes 9220
  253.0 381.0 %copy-start.22 = (f32[1,512]{1,0:T(1,128)S(1)}, f32[1,512]{1,0:T(1,128)}, u32[]{:S(2)}) copy-start(f32[1,512]{1,0:T(1,128)} %get-tuple-element.61) | copy-start | bytes 6148
  253.0 424.3 %all-to-all-start = ((bf16[96,32,512]{2,1,0:T(8,128)(2,1)}), bf16[96,32,512]{2,1,0:T(8,128)(2,1)S(1)}, u32[]{:S(2)}, u32[]{:S(2)}) async-start(bf16[96,32,512]{2,1,0:T(8,128)(2,1)} %pack.1), calls=%async_computation | async-start | bytes 6291456 | tf_op jit(solution)/shard_map/all_to_all | solution.py:650
  259.0 432.2 %all-reduce.4.cloned.1.call-start = ((), (), s32[]{:S(2)}) async-start(), calls=%async_computation.12 | async-start | bytes 3735552 | tf_op jit(solution)/shard_map/psum | solution.py:663
  677.3 1.7 copy-start.1
  691.2 4.4 copy-start.2
  691.2 5.4 copy-start.4
  691.2 6.1 copy-start.5
Sparse Core Ops, SparseCore 0:
  182.1 63.9 reduce-scatter.13
  250.5 102.0 reduce-scatter.7
  357.3 78.1 reduce-scatter.5
  439.4 94.7 reduce-scatter.9
  538.2 95.0 reduce-scatter.11
  636.0 48.4 all-reduce.3

commit v2 on v1

--- a/solution.py
+++ b/solution.py
@@ -324,7 +324,7 @@
 
 def attn_bwd_kernel(
     hgrad_ref, att_ref, qkvp_ref, x_ref, gain_ref, shift_ref, wout_ref, wqkv_ref,
-    pgrad_ref, wqkvg_ref, woutg_ref, obias_ref, qkvb_ref, lng_ref, lns_ref,
+    pgrad_ref, wg_ref, obias_ref, qkvb_ref, lng_ref, lns_ref,
     ags, dqs, wqacc, woacc,
 ):
     g = pl.program_id(0)
@@ -384,8 +384,8 @@
 
     @pl.when(g == 1)
     def _():
-        wqkvg_ref[...] = wqacc[...].astype(BF)
-        woutg_ref[...] = woacc[...].astype(BF)
+        wg_ref[:, : 3 * D] = wqacc[...].astype(BF)
+        wg_ref[:, 3 * D :] = woacc[...].astype(BF)
 
 
 def attn_bwd(hgrad, att, qkvp, x, gain, shift, wout, wqkv):
@@ -405,8 +405,7 @@
         ],
         out_specs=[
             rows,
-            whole((D, 3 * D)),
-            whole((D, D)),
+            whole((D, 4 * D)),
             whole((1, D)),
             whole((1, 3 * D)),
             whole((1, D)),
@@ -414,8 +413,7 @@
         ],
         out_shape=[
             jax.ShapeDtypeStruct((ROWS, D), BF),
-            jax.ShapeDtypeStruct((D, 3 * D), BF),
-            jax.ShapeDtypeStruct((D, D), BF),
+            jax.ShapeDtypeStruct((D, 4 * D), BF),
             jax.ShapeDtypeStruct((1, D), F32),
             jax.ShapeDtypeStruct((1, 3 * D), F32),
             jax.ShapeDtypeStruct((1, D), F32),
@@ -575,6 +573,250 @@
         compiler_params=params(),
         name="mlp_bwd",
     )(egrad, block_in, hidden, gain, shift, we, act, slope, w2, w1)
+
+
+MESH = pl.DeviceIdType.MESH
+
+
+def axis_sizes(dp_count, seq_count):
+    z = 4 if seq_count % 4 == 0 else 1
+    return {"core": 2, "x": dp_count // 2, "y": seq_count // z, "z": z}
+
+
+def cut(dp_count, rows, cols):
+    for a in range(1, dp_count + 1):
+        b = dp_count // a
+        if a * b == dp_count and rows % (16 * a) == 0 and cols % (128 * b) == 0:
+            return a, b
+    raise ValueError("no cut")
+
+
+def chunk_list(dp_count, shapes):
+    chunks = []
+    for at, (rows, cols) in enumerate(shapes):
+        a, b = cut(dp_count, rows, cols)
+        r, c = rows // a, cols // b
+        halves = 2 if r % 32 == 0 and r * c > 32768 else 1
+        for h in range(halves):
+            chunks.append((at, a, b, r, h * (r // halves), r // halves, c))
+    return chunks
+
+
+ORDERS = (("x", "y", "z"), ("y", "x", "z"))
+OWN_DIMS = {"x": 0, "z": 1, "y": 2}
+
+
+def reduce_kernel(sizes, shapes, chunks, *refs):
+    n = len(shapes)
+    ins, outs, refs = refs[:n], refs[n : 2 * n], refs[2 * n :]
+    per = 6
+    bufs = [refs[per * i : per * (i + 1)] for i in range(len(chunks))]
+    local_sem, send_sem, recv_sem = refs[per * len(chunks) :]
+    dp, sq = lax.axis_index("dp"), lax.axis_index("seq")
+    ny = sizes["y"]
+    me = {"core": lax.rem(dp, 2), "x": dp // 2, "y": lax.rem(sq, ny), "z": sq // ny}
+
+    def device(coord):
+        return {"dp": coord["x"] * 2 + coord["core"], "seq": coord["z"] * ny + coord["y"]}
+
+    def peer(axis, d):
+        coord = dict(me)
+        coord[axis] = lax.rem(me[axis] + d, sizes[axis])
+        return coord
+
+    count = 0
+    barrier = pltpu.get_barrier_semaphore()
+    for axis in sizes:
+        for d in range(1, sizes[axis]):
+            pl.semaphore_signal(barrier, inc=1, device_id=device(peer(axis, d)), device_id_type=MESH)
+            count += 1
+    pl.semaphore_wait(barrier, count)
+
+    most = max(sizes.values())
+
+    def copy(i, stage, d, src, dst, coord):
+        slot = (i * 6 + stage) * most + d
+        return pltpu.make_async_remote_copy(
+            src_ref=src,
+            dst_ref=dst,
+            send_sem=send_sem.at[slot],
+            recv_sem=recv_sem.at[slot],
+            device_id=device(coord),
+            device_id_type=MESH,
+        )
+
+    def piece(i, x, core):
+        at, a, b, r, r0, rows, cols = chunks[i]
+        q = x * 2 + core
+        row = (q // b) * r + r0
+        return ins[at].at[
+            :, :, pl.ds(pl.multiple_of(row, 16), rows), pl.ds(pl.multiple_of(lax.rem(q, b) * cols, 128), cols)
+        ]
+
+    def index(done, axis=None, value=None):
+        at = [slice(None)] * 3
+        for name in done:
+            at[OWN_DIMS[name]] = me[name]
+        if axis is not None:
+            at[OWN_DIMS[axis]] = value
+        return tuple(at)
+
+    nx = sizes["x"]
+    loads, sends = [], {}
+    for i in range(len(chunks)):
+        own, recv = bufs[i][:2]
+        sends[i, 0] = []
+        for x in range(nx):
+            sends[i, 0].append(
+                copy(i, 0, x, piece(i, x, 1 - me["core"]), recv.at[x], peer("core", 1))
+            )
+            sends[i, 0][-1].start()
+        load = []
+        for x in range(nx):
+            load.append(
+                pltpu.make_async_copy(piece(i, x, me["core"]), own.at[x], local_sem.at[i * nx + x])
+            )
+            load[-1].start()
+        loads.append(load)
+
+    def add_core(i):
+        own, recv = bufs[i][:2]
+        for x in range(nx):
+            loads[i][x].wait()
+            sends[i, 0][x].wait()
+
+        def body(k, carry):
+            x, z, y = k // (sizes["z"] * ny), lax.rem(k // ny, sizes["z"]), lax.rem(k, ny)
+            own[x, z, y] = own[x, z, y] + recv[x, z, y]
+            return carry
+
+        lax.fori_loop(0, nx * sizes["z"] * ny, body, 0)
+
+    def start(i, stage):
+        order = ORDERS[i % 2]
+        axis, done = order[stage - 1], order[: stage - 1]
+        own, recv = bufs[i][0], bufs[i][1 + stage]
+        sends[i, stage] = []
+        for d in range(1, sizes[axis]):
+            coord = peer(axis, d)
+            sends[i, stage].append(
+                copy(i, stage, d - 1, own.at[index(done, axis, coord[axis])], recv.at[d - 1], coord)
+            )
+            sends[i, stage][-1].start()
+
+    def add(i, stage):
+        order = ORDERS[i % 2]
+        done = order[:stage]
+        own, recv, gathered = bufs[i][0], bufs[i][1 + stage], bufs[i][5]
+        for c in sends[i, stage]:
+            c.wait()
+        left = [name for name in ("x", "z", "y") if name not in done]
+        total = math.prod(sizes[name] for name in left)
+
+        def body(k, carry):
+            at, rest = {name: me[name] for name in done}, k
+            for name in reversed(left):
+                at[name] = lax.rem(rest, sizes[name])
+                rest = rest // sizes[name]
+            here = (at["x"], at["z"], at["y"])
+            there = tuple(at[name] for name in left)
+            value = own[here].astype(F32)
+            for d in range(sizes[order[stage - 1]] - 1):
+                value = value + recv[(d,) + there].astype(F32)
+            if stage == 3:
+                gathered[me["x"] * 2 + me["core"]] = value.astype(BF)
+            else:
+                own[here] = value.astype(BF)
+            return carry
+
+        if total == 1:
+            body(0, 0)
+        else:
+            lax.fori_loop(0, total, body, 0)
+
+    def gather(i, stage):
+        gathered = bufs[i][5]
+        sends[i, stage] = []
+        if stage == 4:
+            q = me["x"] * 2 + me["core"]
+            for d in range(1, nx):
+                sends[i, stage].append(
+                    copy(i, stage, d - 1, gathered.at[q], gathered.at[q], peer("x", d))
+                )
+        else:
+            for x in range(nx):
+                q = x * 2 + me["core"]
+                sends[i, stage].append(
+                    copy(i, stage, x, gathered.at[q], gathered.at[q], peer("core", 1))
+                )
+        for c in sends[i, stage]:
+            c.start()
+
+    def finish(i):
+        at, a, b, r, r0, rows, cols = chunks[i]
+        gathered = bufs[i][5]
+        for c in sends[i, 5]:
+            c.wait()
+        for q in range(a * b):
+            row, col = (q // b) * r + r0, (q % b) * cols
+            outs[at][row : row + rows, col : col + cols] = gathered[q].astype(F32)
+
+    def wait_all(i, stage):
+        for c in sends[i, stage]:
+            c.wait()
+
+    pairs = [[i for i in (2 * p, 2 * p + 1) if i < len(chunks)] for p in range((len(chunks) + 1) // 2)]
+    steps = [
+        lambda i: (add_core(i), start(i, 1)),
+        lambda i: (add(i, 1), start(i, 2)),
+        lambda i: (add(i, 2), start(i, 3)),
+        lambda i: (add(i, 3), gather(i, 4)),
+        lambda i: (wait_all(i, 4), gather(i, 5)),
+        finish,
+    ]
+    for step in range(len(pairs) + len(steps) - 1):
+        for p in range(len(pairs)):
+            if 0 <= step - p < len(steps):
+                for i in pairs[p]:
+                    steps[step - p](i)
+
+
+def reduce_all(arrays):
+    dp_count, seq_count = lax.axis_size("dp"), lax.axis_size("seq")
+    sizes = axis_sizes(dp_count, seq_count)
+    shapes = [(v.shape[0] // seq_count, v.shape[1]) for v in arrays]
+    chunks = chunk_list(dp_count, shapes)
+    nx, ny, nz = sizes["x"], sizes["y"], sizes["z"]
+    views = [
+        v.reshape(nz, ny, rows, cols) for v, (rows, cols) in zip(arrays, shapes, strict=True)
+    ]
+    scratch = []
+    for i, (_, _, _, _, _, rows, cols) in enumerate(chunks):
+        order = ORDERS[i % 2]
+        scratch.append(pltpu.VMEM((nx, nz, ny, rows, cols), BF))
+        scratch.append(pltpu.VMEM((nx, nz, ny, rows, cols), BF))
+        for stage in range(1, 4):
+            done = order[:stage]
+            left = [sizes[name] for name in ("x", "z", "y") if name not in done]
+            scratch.append(pltpu.VMEM((sizes[order[stage - 1]] - 1, *left, rows, cols), BF))
+        scratch.append(pltpu.VMEM((dp_count, rows, cols), BF))
+    slots = len(chunks) * 6 * max(sizes.values())
+    return pl.pallas_call(
+        functools.partial(reduce_kernel, sizes, shapes, chunks),
+        in_specs=[pl.BlockSpec(memory_space=pl.ANY)] * len(arrays),
+        out_specs=[pl.BlockSpec(memory_space=pltpu.VMEM)] * len(arrays),
+        out_shape=[jax.ShapeDtypeStruct(shape, F32) for shape in shapes],
+        scratch_shapes=scratch
+        + [
+            pltpu.SemaphoreType.DMA((len(chunks) * nx,)),
+            pltpu.SemaphoreType.DMA((slots,)),
+            pltpu.SemaphoreType.DMA((slots,)),
+        ],
+        compiler_params=pltpu.CompilerParams(
+            collective_id=0, has_side_effects=True, vmem_limit_bytes=60 * MIB
+        ),
+        name="reduce_all",
+    )(*views)
 
 
 def decoder_codes(keep_index, slots):
@@ -654,29 +896,31 @@
         embed_grad, block_in, hidden, row(ln2_gain), row(ln2_shift), w_embed, active, slope,
         w_fc2, w_fc1,
     )
-    patches_grad, wqkvg, woutg, obias, qkvb, ln1g, ln1s = attn_bwd(
+    patches_grad, wg, obias, qkvb, ln1g, ln1s = attn_bwd(
         hgrad, attended, qkvp, patches, row(ln1_gain), row(ln1_shift), w_out, w_qkv
     )
-    decoder_input = place(seq_count, slots, dec_code, arrived, row(mask_token))
-
-    shares = [
-        lax.psum(lax.psum_scatter(v, "seq", scatter_dimension=0, tiled=True), "dp").astype(F32)
-        for v in (weg, w2g, w1g, woutg, wqkvg)
-    ]
     vectors = [
         ln1g, ln1s, qkvb[:, :D], qkvb[:, 2 * D :], obias, ln2g, ln2s, b1, b2, ebias, mask_rows[:1],
     ]
     packed = jnp.concatenate([v.reshape(seq_count, -1) for v in vectors], axis=1).astype(BF)
-    small = lax.psum(
-        lax.psum_scatter(packed, "seq", scatter_dimension=0, tiled=True), "dp"
-    ).astype(F32).reshape(-1)
+    small_rows = D // seq_count
+    extra = -(-packed.shape[1] // DEC)
+    padded_rows = -(-(small_rows + extra) // 16) * 16
+    packed = jnp.pad(packed, ((0, 0), (0, extra * DEC - packed.shape[1])))
+    tail = jnp.concatenate(
+        [weg.reshape(seq_count, small_rows, DEC), packed.reshape(seq_count, extra, DEC)], axis=1
+    )
+    tail = jnp.pad(tail, ((0, 0), (0, padded_rows - tail.shape[1]), (0, 0)))
+    w1g, w2g, wg, tail = reduce_all([w1g, w2g, wg, tail.reshape(seq_count * padded_rows, DEC)])
+    wqkvg, woutg, weg = wg[:, : 3 * D], wg[:, 3 * D :], tail[:small_rows]
+    small = tail[small_rows:].reshape(-1)
     parts, at = [], 0
     for v in vectors:
         size = v.shape[1] // seq_count
         parts.append(small[at : at + size])
         at += size
     ln1g, ln1s, qb, vb, obias, ln2g, ln2s, b1, b2, ebias, mask_grad = parts
-    weg, w2g, w1g, woutg, wqkvg = shares
+    decoder_input = place(seq_count, slots, dec_code, arrived, row(mask_token))
     return (
         decoder_input,
         patches_grad,

time: 710 us -> 380 us (0.54)
  waiting for transfers between devices: 374 us -> 0.01 us
  Pallas kernels: 228 us -> 325 us
  blocking collectives: 42.4 us -> 0 us
  between operations: 14.8 us -> 1.21 us
    reduce_scatter x5 -> x0, waiting for transfers between devices: 373 us -> none  [local(): lax.psum_scatter(v, 'seq', scatter_dimension=0, tiled=True)]
    pallas_call x0 -> x1, Pallas kernels: none -> 97.9 us  [reduce_all(): pl.pallas_call(functools.partial(reduce_kernel, sizes, shapes, chunks), i...]
    unnamed x1 -> x0, blocking collectives: 35.9 us -> none
  transfers between devices with their start and end apart: 8 -> 2, of which waited for: 4 -> 0; matrix products, arithmetic and copies ran while one was open for 2% -> 5% of each run, Pallas kernels for 23% -> 81%
where the time goes in v2:
time: 380 us; the launch traced here: 376 us
  Pallas kernels  325 us (86%)
  local copies, waits for them, and re-layouts  20.8 us (5%)
  other arithmetic  14.3 us (4%)
  starting transfers between devices  14 us (4%)
    pallas_call x1, Pallas kernels, reduce_all(): pl.pallas_call(functools.partial(reduce_kernel, sizes, shapes, chunks), i...  97.9 us
    pallas_call x1, Pallas kernels, attn_bwd(): pl.pallas_call(attn_bwd_kernel, grid=(2,), in_specs=[rows, rows, pl.Block...  62.9 us
    pallas_call x1, Pallas kernels, mlp_bwd(): pl.pallas_call(mlp_bwd_kernel, grid=(FSTEPS,), in_specs=[whole((ROWS, DEC...  50.6 us
    pallas_call x1, Pallas kernels, attn_fwd(): pl.pallas_call(attn_fwd_kernel, grid=(2,), in_specs=[pl.BlockSpec((HROWS,...  44 us
    pallas_call x1, Pallas kernels, mlp_fwd(): pl.pallas_call(mlp_fwd_kernel, grid=(FSTEPS,), in_specs=[whole((ROWS, D))...  39.3 us
    pallas_call x1, Pallas kernels, place(): pl.pallas_call(functools.partial(place_kernel, seq_count, slots), grid=(s...  10.5 us
    pallas_call x1, Pallas kernels, pick(): pl.pallas_call(functools.partial(pick_kernel, seq_count, slots), grid=(se...  9.01 us
    reduce_sum x1, other arithmetic, decoder_codes(): rank = jnp.sum(below.astype(jnp.int32), axis=0)  8.02 us
  transfers between devices with their start and end apart: 2, of which 0 were waited for; matrix products, arithmetic and copies ran while one was open for 5% of the time, Pallas kernels for 81%

profile of v2, /device:TPU:0, one launch (start us, length us, event | category | flops | bytes accessed | tf_op | source)
XLA Modules:
  0.0 375.7 jit_solution(13585266874083394914)
XLA Ops:
  0.7 0.9 copy.49
  1.8 8.0 %convert_reduce_fusion = (s32[8,28,32]{2,1,0:T(8,128)S(1)}, s32[8,28,32]{2,1,0:T(8,128)S(1)}) fusion(s32[8,28]{1,0:T(8,128)S(1)} %iota_add_fusion.1, s32[49,8,32]{0,2,1:T(8,128)S(1)} %bitcast.19, pred[49,8,32]{0,2,1:T(8,128)(4,1)S(1)} %broadcast_compare_fusion), kind=kLoop, calls=%fused_computation | loop fusion | flops 2444288 | bytes 120960 | tf_op jit(solution)/shard_map/reduce_sum | solution.py:834
  9.8 0.1 mul.61
  10.0 0.1 gt.19
  10.2 0.1 broadcast_in_dim.20
  10.3 0.1 broadcast_in_dim.38
  10.5 0.7 select_select_fusion.code_ref
  11.2 9.0 %pick.1 = (bf16[96,32,512]{2,1,0:T(8,128)(2,1)}, f32[8,512]{1,0:T(8,128)}) custom-call(s32[8,1,896]{2,1,0:T(1,128)} %select_select_fusion.code_ref, bf16[6272,512]{1,0:T(8,128)(2,1)} %dec_ref.1), custom_call_target="tpu_custom_call" | custom-call | tf_op jit(solution)/shard_map/pick/pallas_call | solution.py:121
  20.3 8.0 %all-to-all-start.1 = ((bf16[96,32,512]{2,1,0:T(8,128)(2,1)}), bf16[96,32,512]{2,1,0:T(8,128)(2,1)S(1)}, u32[]{:S(2)}, u32[]{:S(2)}) async-start(bf16[96,32,512]{2,1,0:T(8,128)(2,1)} %get-tuple-element.48), calls=%async_computation.1 | async-start | bytes 6291456 | tf_op jit(solution)/shard_map/all_to_all | solution.py:881
  28.3 0.1 add_select_fusion
  28.4 1.1 convert_reduce_fusion.2
  29.6 0.1 multiply_add_fusion
  29.8 0.7 reshape.339.code_ref
  30.5 0.6 reshape.340.gain_ref
  31.1 0.6 reshape.341.shift_ref
  31.7 0.6 reshape.342.bias_ref
  32.3 0.6 reshape.343.obias_ref
  32.9 0.6 reshape.344.gain_ref
  33.5 0.6 reshape.345.shift_ref
  34.1 0.6 reshape.347.b2_ref
  34.7 44.0 %attn_fwd.1 = (bf16[32,64,2304]{2,1,0:T(8,128)(2,1)}, bf16[1568,768]{1,0:T(8,128)(2,1)}, f32[1568,768]{1,0:T(8,128)}) custom-call(bf16[1568,768]{1,0:T(8,128)(2,1)} %x_ref.3, f32[1,768]{1,0:T(1,128)} %reshape.340.gain_ref, f32[1,768]{1,0:T(1,128)} %reshape.341.shift_ref, bf16[768,2304]{1,0:T(8,128)(2,1)} %wqkv_ref.3, f32[1,2304]{1,0:T(1,128)} %reshape.342.bias_ref, ...), custom_call_target="tpu_custom_call" | custom-call | tf_op jit(solution)/shard_map/attn_fwd/pallas_call | solution.py:297
  78.7 39.3 %mlp_fwd.1 = (bf16[1568,3072]{1,0:T(8,128)(2,1)}, bf16[1568,3072]{1,0:T(8,128)(2,1)}, bf16[1568,768]{1,0:T(8,128)(2,1)}, bf16[1568,512]{1,0:T(8,128)(2,1)}) custom-call(f32[1568,768]{1,0:T(8,128)} %get-tuple-element.46.hidden_ref, f32[1,768]{1,0:T(1,128)} %reshape.344.gain_ref, f32[1,768]{1,0:T(1,128)} %reshape.345.shift_ref, bf16[768,3072]{1,0:T(8,128)(2,1)} %w1_ref.3, ...), custom_call_target="tpu_custom_call" | custom-call | tf_op jit(solution)/shard_map/mlp_fwd/pallas_call | solution.py:466
  118.0 6.0 %pack.1 = bf16[96,32,512]{2,1,0:T(8,128)(2,1)} custom-call(s32[2,1,784]{2,1,0:T(1,128)} %reshape.339.code_ref, bf16[1568,512]{1,0:T(8,128)(2,1)} %get-tuple-element.47.rows_ref), custom_call_target="tpu_custom_call" | custom-call | tf_op jit(solution)/shard_map/pack/pallas_call | solution.py:185
  124.0 1.7 copy-done
  125.7 6.0 %all-to-all-start = ((bf16[96,32,512]{2,1,0:T(8,128)(2,1)}), bf16[96,32,512]{2,1,0:T(8,128)(2,1)}, u32[]{:S(2)}, u32[]{:S(2)}) async-start(bf16[96,32,512]{2,1,0:T(8,128)(2,1)} %pack.1), calls=%async_computation | async-start | bytes 6291456 | tf_op jit(solution)/shard_map/all_to_all | solution.py:892
  131.7 0.7 fusion.4
  132.5 5.3 %unpack.1.egrad_ref = bf16[1568,512]{1,0:T(8,128)(2,1)} custom-call(s32[2,1,784]{2,1,0:T(1,128)} %reshape.339.code_ref, bf16[96,32,512]{2,1,0:T(8,128)(2,1)} %copy-done), custom_call_target="tpu_custom_call" | custom-call | tf_op jit(solution)/shard_map/unpack/pallas_call | solution.py:207
  137.8 50.6 %mlp_bwd.1 = (f32[1568,768]{1,0:T(8,128)}, bf16[768,512]{1,0:T(8,128)(2,1)}, f32[1,512]{1,0:T(1,128)}, bf16[3072,768]{1,0:T(8,128)(2,1)}, f32[1,768]{1,0:T(1,128...) custom-call(bf16[1568,512]{1,0:T(8,128)(2,1)} %unpack.1.egrad_ref, ...), custom_call_target="tpu_custom_call" | custom-call | tf_op jit(solution)/shard_map/mlp_bwd/pallas_call | solution.py:531
  188.4 62.9 %attn_bwd.1 = (bf16[1568,768]{1,0:T(8,128)(2,1)}, bf16[768,3072]{1,0:T(8,128)(2,1)}, f32[1,768]{1,0:T(1,128)}, f32[1,2304]{1,0:T(1,128)}, f32[1,768]{1,0:T(1,128)}, /*index=5*/f32[1,768]{1,0:T(1,128)}) custom-call(f32[1568,768]{1,0:T(8,128)} %get-tuple-element.52.hgrad_ref, bf16[1568,768]{1,0:T(8,128)(2,1)} %get-tuple-element.53.att_ref, ...), custom_call_target="tpu_custom_call" | custom-call | tf_op jit(solution)/shard_map/attn_bwd/pallas_call | solution.py:393
  251.3 0.7 convert.47
  252.1 0.1 reshape.356
  252.3 0.7 convert_reduce_fusion.9
  253.0 0.7 convert_reduce_fusion.8
  253.8 0.7 convert_reduce_fusion.7
  255.1 0.1 concatenate.11
  255.3 1.0 fusion.2
  256.3 97.9 %reduce_all.1 = (f32[96,3072]{1,0:T(8,128)}, f32[384,768]{1,0:T(8,128)}, f32[96,3072]{1,0:T(8,128)}, f32[112,512]{1,0:T(8,128)}) custom-call(bf16[4,2,96,3072]{3,2,1,0:T(8,128)(2,1)} %bitcast.16, bf16[4,2,384,768]{3,2,1,0:T(8,128)(2,1)} %bitcast.15, bf16[4,2,96,3072]{3,2,1,0:T(8,128)(2,1)} %bitcast.17, bf16[4,2,112,512]{3,2,1,0:T(8,128)(2,1)} %bitcast.18), custom_call_target="tpu_custom_call" | custom-call | tf_op jit(solution)/shard_map/reduce_all/pallas_call | solution.py:804
  354.2 2.1 slice.63
  356.4 1.7 slice.66
  358.1 1.6 slice.72
  359.7 0.8 slice_bitcast_fusion
  360.5 0.6 slice.85
  361.1 0.6 fusion.6
  361.7 0.6 fusion.7
  362.3 10.5 %place.1 = bf16[6272,512]{1,0:T(8,128)(2,1)} custom-call(s32[8,1,896]{2,1,0:T(1,128)} %select_select_fusion.code_ref, bf16[96,32,512]{2,1,0:T(8,128)(2,1)} %all-to-all-done.arrived_ref, f32[1,512]{1,0:T(1,128)} %bitcast.25), custom_call_target="tpu_custom_call" | custom-call | tf_op jit(solution)/shard_map/place/pallas_call | solution.py:163
  372.8 1.0 copy.58
  373.8 0.7 copy-done.1
  374.5 1.0 copy.59
  (69 shorter events, 1.6 us)
Async XLA Ops:
  20.2 8.1 %copy-start.4 = (s32[256,49]{0,1:T(8,128)S(1)}, s32[256,49]{0,1:T(8,128)}, u32[]{:S(2)}) copy-start(s32[256,49]{0,1:T(8,128)} %param.20) | copy-start | bytes 150532
  20.2 10.3 %copy-start.6 = (f32[768]{0:T(1024)S(1)}, f32[768]{0:T(1024)}, u32[]{:S(2)}) copy-start(f32[768]{0:T(1024)} %param.21) | copy-start | bytes 9220
  20.2 10.9 %copy-start.7 = (f32[768]{0:T(1024)S(1)}, f32[768]{0:T(1024)}, u32[]{:S(2)}) copy-start(f32[768]{0:T(1024)} %param.22) | copy-start | bytes 9220
  20.2 11.5 %copy-start.12 = (f32[768]{0:T(1024)S(1)}, f32[768]{0:T(1024)}, u32[]{:S(2)}) copy-start(f32[768]{0:T(1024)} %param.25) | copy-start | bytes 9220
  20.2 11.5 %copy-start.13 = (f32[768]{0:T(1024)S(1)}, f32[768]{0:T(1024)}, u32[]{:S(2)}) copy-start(f32[768]{0:T(1024)} %param.24) | copy-start | bytes 9220
  20.2 12.1 %copy-start.8 = (f32[768]{0:T(1024)S(1)}, f32[768]{0:T(1024)}, u32[]{:S(2)}) copy-start(f32[768]{0:T(1024)} %param.27) | copy-start | bytes 9220
  20.2 12.6 %copy-start.9 = (f32[768]{0:T(1024)S(1)}, f32[768]{0:T(1024)}, u32[]{:S(2)}) copy-start(f32[768]{0:T(1024)} %param.28) | copy-start | bytes 9220
  20.2 13.2 %copy-start.10 = (f32[768]{0:T(1024)S(1)}, f32[768]{0:T(1024)}, u32[]{:S(2)}) copy-start(f32[768]{0:T(1024)} %param.29) | copy-start | bytes 9220
  20.2 13.8 %copy-start.11 = (f32[768]{0:T(1024)S(1)}, f32[768]{0:T(1024)}, u32[]{:S(2)}) copy-start(f32[768]{0:T(1024)} %param.33) | copy-start | bytes 9220
  20.3 103.7 %all-to-all-start.1 = ((bf16[96,32,512]{2,1,0:T(8,128)(2,1)}), bf16[96,32,512]{2,1,0:T(8,128)(2,1)S(1)}, u32[]{:S(2)}, u32[]{:S(2)}) async-start(bf16[96,32,512]{2,1,0:T(8,128)(2,1)} %get-tuple-element.48), calls=%async_computation.1 | async-start | bytes 6291456 | tf_op jit(solution)/shard_map/all_to_all | solution.py:881
  124.0 1.7 copy-start
  125.7 236.6 %all-to-all-start = ((bf16[96,32,512]{2,1,0:T(8,128)(2,1)}), bf16[96,32,512]{2,1,0:T(8,128)(2,1)}, u32[]{:S(2)}, u32[]{:S(2)}) async-start(bf16[96,32,512]{2,1,0:T(8,128)(2,1)} %pack.1), calls=%async_computation | async-start | bytes 6291456 | tf_op jit(solution)/shard_map/all_to_all | solution.py:892
  188.4 66.3 %copy-start.5 = (f32[1,3072]{1,0:T(1,128)S(1)}, f32[1,3072]{1,0:T(1,128)}, u32[]{:S(2)}) copy-start(f32[1,3072]{1,0:T(1,128)} %get-tuple-element.66) | copy-start | bytes 36868
  188.4 66.3 %copy-start.16 = (f32[1,768]{1,0:T(1,128)S(1)}, f32[1,768]{1,0:T(1,128)}, u32[]{:S(2)}) copy-start(f32[1,768]{1,0:T(1,128)} %get-tuple-element.64) | copy-start | bytes 9220
  188.4 66.4 %copy-start.15 = (f32[1,768]{1,0:T(1,128)S(1)}, f32[1,768]{1,0:T(1,128)}, u32[]{:S(2)}) copy-start(f32[1,768]{1,0:T(1,128)} %get-tuple-element.65) | copy-start | bytes 9220
  188.4 66.5 %copy-start.14 = (f32[1,768]{1,0:T(1,128)S(1)}, f32[1,768]{1,0:T(1,128)}, u32[]{:S(2)}) copy-start(f32[1,768]{1,0:T(1,128)} %get-tuple-element.67) | copy-start | bytes 9220
  188.4 66.6 %copy-start.17 = (f32[1,512]{1,0:T(1,128)S(1)}, f32[1,512]{1,0:T(1,128)}, u32[]{:S(2)}) copy-start(f32[1,512]{1,0:T(1,128)} %get-tuple-element.68) | copy-start | bytes 6148
  188.4 66.9 %copy-start.3 = (bf16[768,512]{1,0:T(8,128)(2,1)S(1)}, bf16[768,512]{1,0:T(8,128)(2,1)}, u32[]{:S(2)}) copy-start(bf16[768,512]{1,0:T(8,128)(2,1)} %get-tuple-element.59) | copy-start | bytes 2359300
  362.3 10.5 %copy-start.2 = (f32[96,3072]{1,0:T(8,128)S(1)}, f32[96,3072]{1,0:T(8,128)}, u32[]{:S(2)}) copy-start(f32[96,3072]{1,0:T(8,128)} %get-tuple-element.119) | copy-start | bytes 3538948
  372.8 1.7 copy-start.1

commit v3 on v1

--- a/solution.py
+++ b/solution.py
@@ -159,22 +159,6 @@
                 out_ref[pl.ds(pl.multiple_of(at * IMG, IMG), IMG), :] = piece
 
 
-def place(seq_count, slots, code, arrived, mask_token):
-    return pl.pallas_call(
-        functools.partial(place_kernel, seq_count, slots),
-        grid=(seq_count,),
-        in_specs=[
-            pl.BlockSpec((1, 1, code.shape[2]), lambda t: (t, 0, 0)),
-            pl.BlockSpec((slots, IMG, DEC), lambda t: (t, 0, 0)),
-            whole((1, DEC)),
-        ],
-        out_specs=whole((PATCHES * IMG, DEC)),
-        out_shape=jax.ShapeDtypeStruct((PATCHES * IMG, DEC), BF),
-        compiler_params=params(),
-        name="place",
-    )(code, arrived, mask_token)
-
-
 def pack_kernel(code_ref, rows_ref, out_ref):
     count = out_ref.shape[0]
     picked = dot(one_hot(count * HALF, code_ref[0]), rows_ref[...])
@@ -219,34 +203,29 @@
 
 
 UNIT = 4 * HEAD
+PAIR = 2 * HEAD
 
 
 def block_diag(rows):
+    heads = rows.shape[1] // HEAD
     lane_head = lax.broadcasted_iota(jnp.int32, rows.shape, 1) // HEAD
     zero = jnp.zeros_like(rows)
-    return jnp.concatenate([jnp.where(lane_head == h, rows, zero) for h in range(4)], axis=0)
-
-
-def fold_heads(left, right):
-    low = lax.broadcasted_iota(jnp.int32, (PADK, 2 * HEAD), 1) < HEAD
-    return jnp.concatenate(
-        [
-            jnp.where(low, left[:PADK], left[PADK:]),
-            jnp.where(low, right[:PADK], right[PADK:]),
-        ],
-        axis=1,
-    )
-
-
-def soft_cols(key, query_diag):
-    scores = dot(key, query_diag, NT)
-    valid = lax.broadcasted_iota(jnp.int32, scores.shape, 0) < KEEP
+    return jnp.concatenate([jnp.where(lane_head == h, rows, zero) for h in range(heads)], axis=0)
+
+
+def fold_pair(rows):
+    low = lax.broadcasted_iota(jnp.int32, (PADK, PAIR), 1) < HEAD
+    return jnp.where(low, rows[:PADK], rows[PADK:])
+
+
+def soft(scores, axis):
+    valid = lax.broadcasted_iota(jnp.int32, scores.shape, axis) < KEEP
     scores = jnp.where(valid, scores, -1e30)
-    e = jnp.exp(scores - jnp.max(scores, axis=0, keepdims=True))
-    return e * (1.0 / jnp.sum(e, axis=0, keepdims=True))
-
-
-def each_image(image, *refs):
+    e = jnp.exp(scores - jnp.max(scores, axis=axis, keepdims=True))
+    return e * (1.0 / jnp.sum(e, axis=axis, keepdims=True))
+
+
+def each_image(count, image, *refs):
     def group(g, carry):
         base = pl.multiple_of(g * 8 * KEEP, 8)
         views = [ref.at[pl.ds(base, 8 * KEEP + 16)] for ref in refs]
@@ -254,7 +233,7 @@
             image(g * 8 + near, near, *views)
         return carry
 
-    lax.fori_loop(0, HALF // 8, group, 0)
+    lax.fori_loop(0, count // 8, group, 0)
 
 
 def attn_fwd_kernel(
@@ -273,21 +252,20 @@
 
     def image(i, near, qs, ats):
         r0 = near * KEEP
-        for u in range(UNITS):
+        for u in range(HEADS // 2):
             part = []
             for c in range(3):
-                cols = slice(c * D + u * UNIT, c * D + (u + 1) * UNIT)
+                cols = slice(c * D + u * PAIR, c * D + (u + 1) * PAIR)
                 rows = qs[r0 : r0 + PADK, cols].astype(BF)
-                qkvp_ref[i, :, cols] = rows
+                to = c * UNIT + (u % 2) * PAIR
+                qkvp_ref[u // 2, i, :, to : to + PAIR] = rows
                 part.append(rows)
             q, k, v = part
-            probs = soft_cols(k, block_diag(q * BF(0.125))).astype(BF)
-            out = fold_heads(
-                dot(probs[:, :128], v[:, :128], TN), dot(probs[:, 128:], v[:, 128:], TN)
-            )
-            ats[r0 : r0 + 56, u * UNIT : (u + 1) * UNIT] = out[:56]
-
-    each_image(image, qs, ats)
+            probs = soft(dot(block_diag(q * BF(0.125)), k, NT), 1).astype(BF)
+            out = fold_pair(dot(probs, v))
+            ats[r0 : r0 + 56, u * PAIR : (u + 1) * PAIR] = out[:56]
+
+    each_image(HALF, image, qs, ats)
     att = ats[:HROWS, :].astype(BF)
     att_ref[...] = att
     hidden_ref[...] = x_ref[...].astype(F32) + (dot(att, wout_ref[...]) + obias_ref[...])
@@ -307,12 +285,12 @@
             whole((1, D)),
         ],
         out_specs=[
-            pl.BlockSpec((HALF, PADK, 3 * D), lambda g: (g, 0, 0)),
+            pl.BlockSpec((UNITS, HALF, PADK, 3 * UNIT), lambda g: (0, g, 0, 0)),
             pl.BlockSpec((HROWS, D), lambda g: (g, 0)),
             pl.BlockSpec((HROWS, D), lambda g: (g, 0)),
         ],
         out_shape=[
-            jax.ShapeDtypeStruct((IMG, PADK, 3 * D), BF),
+            jax.ShapeDtypeStruct((UNITS, IMG, PADK, 3 * UNIT), BF),
             jax.ShapeDtypeStruct((ROWS, D), BF),
             jax.ShapeDtypeStruct((ROWS, D), F32),
         ],
@@ -320,116 +298,6 @@
         compiler_params=params(),
         name="attn_fwd",
     )(x, gain, shift, wqkv, bias, wout, obias)
-
-
-def attn_bwd_kernel(
-    hgrad_ref, att_ref, qkvp_ref, x_ref, gain_ref, shift_ref, wout_ref, wqkv_ref,
-    pgrad_ref, wqkvg_ref, woutg_ref, obias_ref, qkvb_ref, lng_ref, lns_ref,
-    ags, dqs, wqacc, woacc,
-):
-    g = pl.program_id(0)
-
-    @pl.when(g == 0)
-    def _():
-        wqacc[...] = jnp.zeros_like(wqacc)
-        woacc[...] = jnp.zeros_like(woacc)
-        for ref in (obias_ref, qkvb_ref, lng_ref, lns_ref):
-            ref[...] = jnp.zeros_like(ref)
-
-    branch = hgrad_ref[...].astype(BF)
-    obias_ref[...] += col_sum(branch.astype(F32))
-    woacc[...] += dot(att_ref[...], branch, TN)
-    ags[:HROWS, :] = dot(branch, wout_ref[...], NT)
-    ags[HROWS:, :] = jnp.zeros((16, D), F32)
-
-    def image(i, near, ags, dqs):
-        r0 = near * KEEP
-        valid = lax.broadcasted_iota(jnp.int32, (PADK, UNIT), 0) < KEEP
-        for u in range(UNITS):
-            q, k, v = (
-                qkvp_ref[i, :, c * D + u * UNIT : c * D + (u + 1) * UNIT] for c in range(3)
-            )
-            q_diag = block_diag(q * BF(0.125))
-            probs = soft_cols(k, q_diag)
-            probs_in = probs.astype(BF)
-            agrad = jnp.where(
-                valid, ags[r0 : r0 + PADK, u * UNIT : (u + 1) * UNIT], 0.0
-            ).astype(BF)
-            a_diag = block_diag(agrad)
-            pgrad = dot(v, a_diag, NT)
-            vgrad = dot(probs_in, a_diag)
-            inner = jnp.sum(probs * pgrad, axis=0, keepdims=True)
-            sgrad = (probs * (pgrad - inner)).astype(BF)
-            kgrad = dot(sgrad, q_diag)
-            qgrad = 0.125 * fold_heads(
-                dot(sgrad[:, :128], k[:, :128], TN), dot(sgrad[:, 128:], k[:, 128:], TN)
-            )
-            for c, grad in enumerate((qgrad, kgrad, vgrad)):
-                dqs[r0 : r0 + 56, c * D + u * UNIT : c * D + (u + 1) * UNIT] = grad[:56]
-
-    each_image(image, ags, dqs)
-    unit, inv = norm(x_ref[...].astype(F32))
-    first = (unit * gain_ref[...] + shift_ref[...]).astype(BF)
-    fgrad = None
-    for c in range(3):
-        cols = slice(c * D, (c + 1) * D)
-        grad = dqs[:HROWS, cols].astype(BF)
-        qkvb_ref[:, cols] += col_sum(grad.astype(F32))
-        wqacc[:, cols] += dot(first, grad, TN)
-        term = dot(grad, wqkv_ref[:, cols], NT)
-        fgrad = term if fgrad is None else fgrad + term
-    lng_ref[...] += col_sum(fgrad * unit)
-    lns_ref[...] += col_sum(fgrad)
-    pgrad_ref[...] = (hgrad_ref[...] + norm_back(unit, inv, fgrad, gain_ref[...])).astype(BF)
-
-    @pl.when(g == 1)
-    def _():
-        wqkvg_ref[...] = wqacc[...].astype(BF)
-        woutg_ref[...] = woacc[...].astype(BF)
-
-
-def attn_bwd(hgrad, att, qkvp, x, gain, shift, wout, wqkv):
-    rows = pl.BlockSpec((HROWS, D), lambda g: (g, 0))
-    return pl.pallas_call(
-        attn_bwd_kernel,
-        grid=(2,),
-        in_specs=[
-            rows,
-            rows,
-            pl.BlockSpec((HALF, PADK, 3 * D), lambda g: (g, 0, 0)),
-            rows,
-            whole((1, D)),
-            whole((1, D)),
-            whole((D, D)),
-            whole((D, 3 * D)),
-        ],
-        out_specs=[
-            rows,
-            whole((D, 3 * D)),
-            whole((D, D)),
-            whole((1, D)),
-            whole((1, 3 * D)),
-            whole((1, D)),
-            whole((1, D)),
-        ],
-        out_shape=[
-            jax.ShapeDtypeStruct((ROWS, D), BF),
-            jax.ShapeDtypeStruct((D, 3 * D), BF),
-            jax.ShapeDtypeStruct((D, D), BF),
-            jax.ShapeDtypeStruct((1, D), F32),
-            jax.ShapeDtypeStruct((1, 3 * D), F32),
-            jax.ShapeDtypeStruct((1, D), F32),
-            jax.ShapeDtypeStruct((1, D), F32),
-        ],
-        scratch_shapes=[
-            pltpu.VMEM((HROWS + 16, D), F32),
-            pltpu.VMEM((HROWS + 16, 3 * D), F32),
-            pltpu.VMEM((D, 3 * D), F32),
-            pltpu.VMEM((D, D), F32),
-        ],
-        compiler_params=params(),
-        name="attn_bwd",
-    )(hgrad, att, qkvp, x, gain, shift, wout, wqkv)
 
 
 FTILE = 512
@@ -575,6 +443,617 @@
         compiler_params=params(),
         name="mlp_bwd",
     )(egrad, block_in, hidden, gain, shift, we, act, slope, w2, w1)
+
+
+MESH = pl.DeviceIdType.MESH
+ORDERS = (("x", "y", "z"), ("y", "x", "z"))
+DIMS = {"x": 0, "z": 1, "y": 2}
+VROWS = 16
+
+
+def axis_sizes(dp_count, seq_count):
+    z = 4 if seq_count % 4 == 0 else 1
+    return {"core": 2, "x": dp_count // 2, "y": seq_count // z, "z": z}
+
+
+def cut(dp_count, rows, cols):
+    for padded in range(rows, rows + 256, 16):
+        for a in range(1, dp_count + 1):
+            b = dp_count // a
+            if a * b == dp_count and padded % (16 * a) == 0 and cols % (128 * b) == 0:
+                return a, b, padded
+    raise ValueError("no cut")
+
+
+class Chunk:
+    def __init__(self, dp_count, rows, cols, half, halves, order):
+        self.a, self.b, self.padded = cut(dp_count, rows, cols)
+        self.r, self.cols = self.padded // self.a, cols // self.b
+        self.rows = self.r // halves
+        self.r0 = half * self.rows
+        self.order = ORDERS[order]
+
+    def scratch(self, sizes):
+        dims = [sizes[name] for name in ("x", "z", "y")]
+        shapes = [(*dims, self.rows, self.cols)] * 2
+        for stage in range(1, 4):
+            left = [sizes[name] for name in ("x", "z", "y") if name not in self.order[:stage]]
+            shapes.append((sizes[self.order[stage - 1]] - 1, *left, self.rows, self.cols))
+        shapes.append((sizes["x"] * 2, self.rows, self.cols))
+        return [pltpu.VMEM(shape, BF) for shape in shapes]
+
+
+def halves_of(dp_count, rows, cols):
+    a, _, padded = cut(dp_count, rows, cols)
+    return 2 if (padded // a) % 32 == 0 else 1
+
+
+def chunk_table(dp_count, seq_count):
+    table = {}
+    for name, rows, cols in (("fc2", FF, D), ("fc1", D, FF)):
+        rows //= seq_count
+        halves = halves_of(dp_count, rows, cols)
+        for h in range(halves):
+            table[f"{name}_{h}"] = Chunk(dp_count, rows, cols, h, halves, h)
+    table["embed"] = Chunk(dp_count, D // seq_count, DEC, 0, 1, 0)
+    for i, name in enumerate(("out", "unit_0", "unit_1", "unit_2")):
+        table[name] = Chunk(dp_count, D // seq_count, D, 0, 1, (i + 1) % 2)
+    return table
+
+
+class Net:
+    def __init__(self, sizes, send_sem, recv_sem):
+        self.sizes, self.send_sem, self.recv_sem = sizes, send_sem, recv_sem
+        self.used = 0
+        dp, sq = lax.axis_index("dp"), lax.axis_index("seq")
+        ny = sizes["y"]
+        self.me = {"core": lax.rem(dp, 2), "x": dp // 2, "y": lax.rem(sq, ny), "z": sq // ny}
+
+    def device(self, axis, value):
+        coord = dict(self.me)
+        coord[axis] = value
+        return {
+            "dp": coord["x"] * 2 + coord["core"],
+            "seq": coord["z"] * self.sizes["y"] + coord["y"],
+        }
+
+    def peer(self, axis, d):
+        return lax.rem(self.me[axis] + d, self.sizes[axis])
+
+    def barrier(self):
+        sem, count = pltpu.get_barrier_semaphore(), 0
+        for axis, size in self.sizes.items():
+            for d in range(1, size):
+                pl.semaphore_signal(
+                    sem, inc=1, device_id=self.device(axis, self.peer(axis, d)), device_id_type=MESH
+                )
+                count += 1
+        pl.semaphore_wait(sem, count)
+
+    def copy(self, src, dst, axis, value):
+        slot = self.used
+        self.used += 1
+        c = pltpu.make_async_remote_copy(
+            src_ref=src,
+            dst_ref=dst,
+            send_sem=self.send_sem.at[slot],
+            recv_sem=self.recv_sem.at[slot],
+            device_id=self.device(axis, value),
+            device_id_type=MESH,
+        )
+        c.start()
+        return c
+
+
+class Sum:
+    def __init__(self, net, chunk, source, bufs, local_sems, out):
+        self.net, self.chunk, self.source, self.out = net, chunk, source, out
+        self.own, self.recv, self.gathered = bufs[0], bufs[1:5], bufs[5]
+        self.local_sems = local_sems
+        self.at = 0
+        self.copies, self.loads = [], []
+
+    def next(self):
+        steps = (self.core, self.first, self.second, self.third, self.spread_x, self.spread_core, self.leave)
+        steps[self.at]()
+        self.at += 1
+
+    def wait(self):
+        for c in self.copies:
+            c.wait()
+        self.copies = []
+
+    def piece(self, x, core):
+        k = self.chunk
+        q = x * 2 + core
+        row = pl.multiple_of((q // k.b) * k.r + k.r0, 16)
+        col = pl.multiple_of(lax.rem(q, k.b) * k.cols, 128)
+        return self.source.at[:, :, pl.ds(row, k.rows), pl.ds(col, k.cols)]
+
+    def core(self):
+        net = self.net
+        for x in range(net.sizes["x"]):
+            other = net.peer("core", 1)
+            self.copies.append(net.copy(self.piece(x, other), self.recv[0].at[x], "core", other))
+        for x in range(net.sizes["x"]):
+            load = pltpu.make_async_copy(
+                self.piece(x, net.me["core"]), self.own.at[x], self.local_sems[x]
+            )
+            load.start()
+            self.loads.append(load)
+
+    def first(self):
+        for load in self.loads:
+            load.wait()
+        self.wait()
+        self.add(0)
+        self.start(1)
+
+    def second(self):
+        self.wait()
+        self.add(1)
+        self.start(2)
+
+    def third(self):
+        self.wait()
+        self.add(2)
+        self.start(3)
+
+    def start(self, stage):
+        net, order = self.net, self.chunk.order
+        axis, done = order[stage - 1], order[: stage - 1]
+        for d in range(1, net.sizes[axis]):
+            value = net.peer(axis, d)
+            at = [slice(None)] * 3
+            for name in done:
+                at[DIMS[name]] = net.me[name]
+            at[DIMS[axis]] = value
+            self.copies.append(
+                net.copy(self.own.at[tuple(at)], self.recv[stage].at[d - 1], axis, value)
+            )
+
+    def add(self, stage):
+        sizes, me = self.net.sizes, self.net.me
+        done = self.chunk.order[:stage]
+        left = [name for name in ("x", "z", "y") if name not in done]
+        terms = 1 if stage == 0 else sizes[done[-1]] - 1
+
+        def body(k, carry):
+            at, rest = {name: me[name] for name in done}, k
+            for name in reversed(left):
+                at[name] = lax.rem(rest, sizes[name])
+                rest = rest // sizes[name]
+            here = (at["x"], at["z"], at["y"])
+            there = tuple(at[name] for name in left)
+            if terms == 1 and stage < 3:
+                other = self.recv[stage][there if stage == 0 else (0,) + there]
+                self.own[here] = self.own[here] + other
+                return carry
+            value = self.own[here].astype(F32)
+            for d in range(terms):
+                value = value + self.recv[stage][(d,) + there].astype(F32)
+            if stage == 3:
+                self.gathered[me["x"] * 2 + me["core"]] = value.astype(BF)
+            else:
+                self.own[here] = value.astype(BF)
+            return carry
+
+        total = math.prod(sizes[name] for name in left)
+        if total == 1:
+            body(0, 0)
+        else:
+            lax.fori_loop(0, total, body, 0)
+
+    def spread_x(self):
+        self.wait()
+        self.add(3)
+        net = self.net
+        mine = self.gathered.at[net.me["x"] * 2 + net.me["core"]]
+        for d in range(1, net.sizes["x"]):
+            self.copies.append(net.copy(mine, mine, "x", net.peer("x", d)))
+
+    def spread_core(self):
+        self.wait()
+        net = self.net
+        for x in range(net.sizes["x"]):
+            mine = self.gathered.at[x * 2 + net.me["core"]]
+            self.copies.append(net.copy(mine, mine, "core", net.peer("core", 1)))
+
+    def leave(self):
+        self.wait()
+        store = pltpu.make_async_copy(self.gathered, self.out, self.local_sems[0])
+        store.start()
+        self.loads = [store]
+
+    def end(self):
+        while self.at < 7:
+            self.next()
+        self.loads[0].wait()
+
+
+class VectorSum:
+    def __init__(self, net, value, slots):
+        self.net, self.value, self.slots = net, value, slots
+        self.left = [name for name, size in net.sizes.items() if size > 1]
+        self.copies = []
+
+    def next(self):
+        if self.copies:
+            for c in self.copies:
+                c.wait()
+            total = self.now[0]
+            for i in range(1, self.net.sizes[self.axis]):
+                total = total + self.now[i]
+            self.value[...] = total
+            self.copies = []
+        if self.left:
+            net, self.axis = self.net, self.left.pop(0)
+            self.now = self.slots[self.axis]
+            mine = self.now.at[net.me[self.axis]]
+            self.now[net.me[self.axis]] = self.value[...]
+            for d in range(1, net.sizes[self.axis]):
+                self.copies.append(net.copy(mine, mine, self.axis, net.peer(self.axis, d)))
+
+    def end(self):
+        while self.left or self.copies:
+            self.next()
+
+
+PROWS = ROWS + 16
+SLOT = {"out": 0, "unit_0": 1, "unit_1": 2, "unit_2": 0}
+
+
+def attn_unit_back(u, half, qbuf, slot, ags, dqs):
+    def image(i, near, ags, dqs):
+        r0 = near * KEEP
+        valid = lax.broadcasted_iota(jnp.int32, (PADK, UNIT), 0) < KEEP
+        q, k, v = (qbuf[slot, i, :, c * UNIT : (c + 1) * UNIT] for c in range(3))
+        q_diag = block_diag(q * BF(0.125))
+        probs = soft(dot(k, q_diag, NT), 0)
+        probs_in = probs.astype(BF)
+        agrad = jnp.where(valid, ags[r0 : r0 + PADK, u * UNIT : (u + 1) * UNIT], 0.0).astype(BF)
+        a_diag = block_diag(agrad)
+        pgrad = dot(v, a_diag, NT)
+        inner = jnp.sum(probs * pgrad, axis=0, keepdims=True)
+        sgrad = (probs * (pgrad - inner)).astype(BF)
+        whole_q = dot(sgrad, k, TN)
+        qgrad = 0.125 * jnp.concatenate(
+            [
+                fold_pair(whole_q[e * 2 * PADK : (e + 1) * 2 * PADK, e * PAIR : (e + 1) * PAIR])
+                for e in range(2)
+            ],
+            axis=1,
+        )
+        for c, grad in enumerate((qgrad, dot(sgrad, q_diag), dot(probs_in, a_diag))):
+            dqs[r0 : r0 + 56, c * UNIT : (c + 1) * UNIT] = grad[:56]
+
+    rows = pl.ds(half * HROWS, HROWS + 16)
+    each_image(HALF, image, ags.at[rows], dqs.at[rows])
+
+
+def back_kernel(sizes, table, *refs):
+    names = list(table)
+    (
+        hgrad_in, att_in, qkvp_in, x_in, wout_in, wqkv_in, w2g_in, w1g_in, weg_in,
+        gain_ref, shift_ref, ln2g_ref, ln2s_ref, b2_ref, b1_ref, ebias_ref, mask_ref,
+    ) = refs[:17]
+    pgrad_out, vec_ref = refs[17:19]
+    outs, refs = refs[19 : 19 + len(names)], refs[19 + len(names) :]
+    (
+        wide_a, ags, dqs, tall, qbuf, wout, wqkv, rows_b, wgs, load_sem, send_sem, recv_sem, local_sem,
+    ) = refs[:13]
+    refs = refs[13:]
+    vec_slots = {name: refs[i] for i, name in enumerate(sizes)}
+    refs = refs[len(sizes) :]
+
+    net = Net(sizes, send_sem, recv_sem)
+    net.barrier()
+    sources = {"fc2": w2g_in, "fc1": w1g_in, "embed": weg_in}
+    sums = {}
+    for i, name in enumerate(names):
+        key = name.split("_")[0]
+        source = wgs.at[SLOT[name]] if name in SLOT else sources[key]
+        sums[name] = Sum(
+            net,
+            table[name],
+            source,
+            refs[6 * i : 6 * (i + 1)],
+            [local_sem.at[i * sizes["x"] + x] for x in range(sizes["x"])],
+            outs[i],
+        )
+    fc2 = [sums[n] for n in names if n.startswith("fc2")]
+    fc1 = [sums[n] for n in names if n.startswith("fc1")]
+    embed, out = sums["embed"], sums["out"]
+    units = [sums[f"unit_{u}"] for u in range(UNITS)]
+
+    def each(*items):
+        for item in items:
+            item.next()
+
+    def load(src, dst, slot):
+        c = pltpu.make_async_copy(src, dst, load_sem.at[slot])
+        c.start()
+        return c
+
+    hg_load = load(hgrad_in, wide_a, 0)
+    wout_load = load(wout_in, wout, 1)
+    att_load = load(att_in, tall, 2)
+    each(*fc2)
+    q_loads = []
+
+    def load_next():
+        k = len(q_loads)
+        if k < 2 * UNITS:
+            part = qkvp_in.at[k // 2, pl.ds((k % 2) * HALF, HALF)]
+            q_loads.append(load(part, qbuf.at[k % 2], 10 + k))
+
+    load_next()
+    wqkv_load = load(wqkv_in, wqkv, 5)
+    each(*fc1, embed)
+
+    blocks = sizes["y"] * sizes["z"]
+    block_rows = D // blocks
+
+    def put_grad(slot, cols, value):
+        for t in range(blocks):
+            wgs[slot, t // sizes["y"], t % sizes["y"], :block_rows, cols] = value[
+                t * block_rows : (t + 1) * block_rows
+            ].astype(BF)
+
+    if table["out"].padded > block_rows:
+        pad = table["out"].padded - block_rows
+        wgs[:, :, :, block_rows:, :] = jnp.zeros((3, sizes["z"], sizes["y"], pad, D), BF)
+
+    vec_ref[...] = jnp.zeros_like(vec_ref)
+    hg_load.wait()
+    wout_load.wait()
+    halves = [slice(0, HROWS), slice(HROWS, ROWS)]
+    for rows in halves:
+        branch = wide_a[rows, :].astype(BF)
+        rows_b[rows, :] = branch
+        vec_ref[4:5] += col_sum(branch.astype(F32))
+        ags[rows, :] = dot(branch, wout[...], NT)
+    ags[ROWS:, :] = jnp.zeros((PROWS - ROWS, D), F32)
+    att_load.wait()
+    for c in range(3):
+        cols = slice(c * UNIT, (c + 1) * UNIT)
+        put_grad(0, cols, dot(tall[...], rows_b[:, cols], TN))
+    x_load = load(x_in, rows_b, 3)
+    each(out)
+    each(*fc2)
+    x_load.wait()
+    for rows in halves:
+        unit, _ = norm(rows_b[rows, :].astype(F32))
+        tall[rows, :] = (unit * gain_ref[...] + shift_ref[...]).astype(BF)
+
+    def unit_products(u):
+        for c in range(3):
+            rows_b[:, c * UNIT : (c + 1) * UNIT] = dqs[:ROWS, c * UNIT : (c + 1) * UNIT].astype(BF)
+        for c in range(3):
+            cols = slice(c * UNIT, (c + 1) * UNIT)
+            put_grad(SLOT[f"unit_{u}"], cols, dot(tall[...], rows_b[:, cols], TN))
+        for c, row in ((0, 2), (2, 3)):
+            vec_ref[row : row + 1, u * UNIT : (u + 1) * UNIT] = col_sum(
+                rows_b[:, c * UNIT : (c + 1) * UNIT].astype(F32)
+            )
+
+    def unit_first_grad(u):
+        for rows in halves:
+            total = None
+            for c in range(3):
+                weight = wqkv[:, c * D + u * UNIT : c * D + (u + 1) * UNIT]
+                term = dot(rows_b[rows, c * UNIT : (c + 1) * UNIT], weight, NT)
+                total = term if total is None else total + term
+            wide_a[rows, :] = total if u == 0 else wide_a[rows, :] + total
+
+    def unit_step(u):
+        for half in range(2):
+            q_loads[2 * u + half].wait()
+            load_next()
+            attn_unit_back(u, half, qbuf, half, ags, dqs)
+
+    unit_step(0)
+    each(*fc1, embed)
+    unit_products(0)
+    each(units[0])
+    wqkv_load.wait()
+    unit_first_grad(0)
+    each(out)
+    unit_step(1)
+    each(*fc2)
+    unit_products(1)
+    each(units[1])
+    unit_first_grad(1)
+    each(units[0])
+    unit_step(2)
+    hg_again = load(hgrad_in, ags.at[pl.ds(0, ROWS)], 8)
+    each(*fc1, embed, out)
+    unit_products(2)
+    each(units[2])
+    each(*fc2)
+    each(units[1])
+    unit_first_grad(2)
+    x_again = load(x_in, rows_b, 6)
+    each(units[2])
+    each(units[0])
+    hg_again.wait()
+    x_again.wait()
+    stores = []
+    for h, rows in enumerate(halves):
+        unit, inv = norm(rows_b[rows, :].astype(F32))
+        grad = wide_a[rows, :]
+        vec_ref[0:1] += col_sum(grad * unit)
+        vec_ref[1:2] += col_sum(grad)
+        tall[rows, :] = (ags[rows, :] + norm_back(unit, inv, grad, gain_ref[...])).astype(BF)
+    stores.append(load(tall, pgrad_out, 9))
+    vec_ref[5:6] = ln2g_ref[...]
+    vec_ref[6:7] = ln2s_ref[...]
+    vec_ref[7:8] = b2_ref[...]
+    for i in range(4):
+        vec_ref[8 + i : 9 + i] = b1_ref[:, i * D : (i + 1) * D]
+    vec_ref[12:13, :DEC] = ebias_ref[...]
+    vec_ref[13:14, :DEC] = mask_ref[:1]
+    vec = VectorSum(net, vec_ref, vec_slots)
+    each(vec)
+    each(*fc1, embed, out)
+    each(*fc2)
+    each(vec)
+    each(units[1])
+    each(units[2])
+    each(units[0])
+    each(*fc1, embed, out)
+    each(vec)
+    each(*fc2)
+    each(units[1])
+    each(units[2])
+    each(units[0])
+    each(vec)
+    each(*fc1, embed, out)
+    each(*fc2)
+    each(units[1])
+    each(units[2])
+    each(units[0])
+    vec.end()
+    for item in sums.values():
+        item.end()
+    for store in stores:
+        store.wait()
+
+
+def attn_back_and_sums(
+    hgrad, att, qkvp, x, wout, wqkv, w2g, w1g, weg, gain, shift, ln2g, ln2s, b2, b1, ebias, mask_rows,
+):
+    dp_count, seq_count = lax.axis_size("dp"), lax.axis_size("seq")
+    sizes = axis_sizes(dp_count, seq_count)
+    table = chunk_table(dp_count, seq_count)
+    nz, ny = sizes["z"], sizes["y"]
+    blocked = lambda v: v.reshape(nz, ny, v.shape[0] // seq_count, v.shape[1])
+    weg = weg.reshape(nz, ny, D // seq_count, DEC)
+    pad = table["embed"].padded - D // seq_count
+    if pad:
+        weg = jnp.pad(weg, ((0, 0), (0, 0), (0, pad), (0, 0)))
+    scratch = [
+        pltpu.VMEM((ROWS, D), F32),
+        pltpu.VMEM((PROWS, D), F32),
+        pltpu.VMEM((PROWS, D), F32),
+        pltpu.VMEM((ROWS, D), BF),
+        pltpu.VMEM((2, HALF, PADK, 3 * UNIT), BF),
+        pltpu.VMEM((D, D), BF),
+        pltpu.VMEM((D, 3 * D), BF),
+        pltpu.VMEM((ROWS, D), BF),
+        pltpu.VMEM((3, nz, ny, table["out"].padded, D), BF),
+        pltpu.SemaphoreType.DMA((16,)),
+    ]
+    copies = sum(sizes["x"] * 3 + sizes["y"] + sizes["z"] for _ in table)
+    copies += sum(sizes.values())
+    scratch += [
+        pltpu.SemaphoreType.DMA((copies,)),
+        pltpu.SemaphoreType.DMA((copies,)),
+        pltpu.SemaphoreType.DMA((len(table) * sizes["x"],)),
+    ]
+    scratch += [pltpu.VMEM((size, VROWS, D), F32) for size in sizes.values()]
+    for chunk in table.values():
+        scratch += chunk.scratch(sizes)
+    anywhere = pl.BlockSpec(memory_space=pl.ANY)
+    vmem = pl.BlockSpec(memory_space=pltpu.VMEM)
+    outs = pl.pallas_call(
+        functools.partial(back_kernel, sizes, table),
+        in_specs=[anywhere] * 9 + [vmem] * 8,
+        out_specs=[anywhere, vmem] + [anywhere] * len(table),
+        out_shape=[
+            jax.ShapeDtypeStruct((ROWS, D), BF),
+            jax.ShapeDtypeStruct((VROWS, D), F32),
+        ]
+        + [jax.ShapeDtypeStruct((dp_count, c.rows, c.cols), BF) for c in table.values()],
+        scratch_shapes=scratch,
+        compiler_params=pltpu.CompilerParams(
+            collective_id=0, has_side_effects=True, vmem_limit_bytes=63 * MIB
+        ),
+        name="attn_back_and_sums",
+    )(
+        hgrad, att, qkvp, x, wout, wqkv, blocked(w2g), blocked(w1g), weg,
+        gain, shift, ln2g, ln2s, b2, b1, ebias, mask_rows,
+    )
+    return outs[0], outs[1], outs[2:]
+
+
+def finish_kernel(seq_count, slots, table, *refs):
+    code_ref, arrived_ref, mask_ref, vec_ref = refs[:4]
+    parts, refs = refs[4 : 4 + len(table)], refs[4 + len(table) :]
+    out_ref, w2_ref, w1_ref, we_ref, wo_ref, wqkv_ref, rows_ref, b1_ref, dec_ref = refs
+    t = pl.program_id(0)
+    place_kernel(seq_count, slots, code_ref, arrived_ref, mask_ref, out_ref)
+
+    @pl.when(t == 0)
+    def _():
+        def pieces(name):
+            chunk, ref = table[name], parts[list(table).index(name)]
+            for q in range(chunk.a * chunk.b):
+                row, col = (q // chunk.b) * chunk.r + chunk.r0, (q % chunk.b) * chunk.cols
+                yield row, col, ref[q].astype(F32)
+
+        for name, ref in (("fc2", w2_ref), ("fc1", w1_ref), ("embed", we_ref), ("out", wo_ref)):
+            for key in table:
+                if key.split("_")[0] == name:
+                    for row, col, value in pieces(key):
+                        rows = min(value.shape[0], ref.shape[0] - row)
+                        if rows > 0:
+                            ref[row : row + rows, col : col + value.shape[1]] = value[:rows]
+        for u in range(UNITS):
+            for row, col, value in pieces(f"unit_{u}"):
+                rows = min(value.shape[0], wqkv_ref.shape[0] - row)
+                if rows > 0:
+                    for i in range(value.shape[1] // 128):
+                        c, within = (col + i * 128) // UNIT, (col + i * 128) % UNIT
+                        to = c * D + u * UNIT + within
+                        wqkv_ref[row : row + rows, to : to + 128] = value[
+                            :rows, i * 128 : (i + 1) * 128
+                        ]
+
+        me = lax.axis_index("seq")
+
+        def mine(row, size, first):
+            shift = lax.rem(D - first, D)
+            return pltpu.roll(vec_ref[row : row + 8], shift, 1)[:, :size]
+
+        rows_ref[...] = mine(0, D // seq_count, me * (D // seq_count))
+        per = seq_count // 4
+        chosen = mine(8, FF // seq_count, lax.rem(me, per) * (FF // seq_count))
+        at = lax.broadcasted_iota(jnp.int32, chosen.shape, 0)
+        b1_ref[...] = jnp.sum(jnp.where(at == me // per, chosen, 0.0), axis=0, keepdims=True)
+        dec_ref[...] = mine(8, DEC // seq_count, me * (DEC // seq_count))
+
+
+def finish(seq_count, slots, code, arrived, mask_token, vec, parts, table):
+    def share(rows, cols):
+        return jax.ShapeDtypeStruct((rows // seq_count, cols), F32)
+
+    out_shape = [
+        jax.ShapeDtypeStruct((PATCHES * IMG, DEC), BF),
+        share(FF, D),
+        share(D, FF),
+        share(D, DEC),
+        share(D, D),
+        share(D, 3 * D),
+        jax.ShapeDtypeStruct((8, D // seq_count), F32),
+        jax.ShapeDtypeStruct((1, FF // seq_count), F32),
+        jax.ShapeDtypeStruct((8, DEC // seq_count), F32),
+    ]
+    return pl.pallas_call(
+        functools.partial(finish_kernel, seq_count, slots, table),
+        grid=(seq_count,),
+        in_specs=[
+            pl.BlockSpec((1, 1, code.shape[2]), lambda t: (t, 0, 0)),
+            pl.BlockSpec((slots, IMG, DEC), lambda t: (t, 0, 0)),
+            whole((1, DEC)),
+            whole(vec.shape),
+        ]
+        + [whole(p.shape) for p in parts],
+        out_specs=[whole(s.shape) for s in out_shape],
+        out_shape=out_shape,
+        compiler_params=params(),
+        name="finish",
+    )(code, arrived, mask_token, vec, *parts)
 
 
 def decoder_codes(keep_index, slots):
@@ -654,29 +1133,16 @@
         embed_grad, block_in, hidden, row(ln2_gain), row(ln2_shift), w_embed, active, slope,
         w_fc2, w_fc1,
     )
-    patches_grad, wqkvg, woutg, obias, qkvb, ln1g, ln1s = attn_bwd(
-        hgrad, attended, qkvp, patches, row(ln1_gain), row(ln1_shift), w_out, w_qkv
+    patches_grad, vec, parts = attn_back_and_sums(
+        hgrad, attended, qkvp, patches, w_out, w_qkv, w2g, w1g, weg,
+        row(ln1_gain), row(ln1_shift), ln2g, ln2s, b2, b1, ebias, mask_rows,
     )
-    decoder_input = place(seq_count, slots, dec_code, arrived, row(mask_token))
-
-    shares = [
-        lax.psum(lax.psum_scatter(v, "seq", scatter_dimension=0, tiled=True), "dp").astype(F32)
-        for v in (weg, w2g, w1g, woutg, wqkvg)
-    ]
-    vectors = [
-        ln1g, ln1s, qkvb[:, :D], qkvb[:, 2 * D :], obias, ln2g, ln2s, b1, b2, ebias, mask_rows[:1],
-    ]
-    packed = jnp.concatenate([v.reshape(seq_count, -1) for v in vectors], axis=1).astype(BF)
-    small = lax.psum(
-        lax.psum_scatter(packed, "seq", scatter_dimension=0, tiled=True), "dp"
-    ).astype(F32).reshape(-1)
-    parts, at = [], 0
-    for v in vectors:
-        size = v.shape[1] // seq_count
-        parts.append(small[at : at + size])
-        at += size
-    ln1g, ln1s, qb, vb, obias, ln2g, ln2s, b1, b2, ebias, mask_grad = parts
-    weg, w2g, w1g, woutg, wqkvg = shares
+    table = chunk_table(lax.axis_size("dp"), seq_count)
+    decoder_input, w2g, w1g, weg, woutg, wqkvg, rows, b1, dec_rows = finish(
+        seq_count, slots, dec_code, arrived, row(mask_token), vec, parts, table
+    )
+    ln1g, ln1s, qb, vb, obias, ln2g, ln2s, b2 = (rows[i] for i in range(8))
+    b1, ebias, mask_grad = b1[0], dec_rows[4], dec_rows[5]
     return (
         decoder_input,
         patches_grad,

time: 710 us -> 317 us (0.45)
  waiting for transfers between devices: 374 us -> 0.01 us
  Pallas kernels: 228 us -> 275 us
  blocking collectives: 42.4 us -> 0 us
  between operations: 14.8 us -> 1.08 us
    reduce_scatter x5 -> x0, waiting for transfers between devices: 373 us -> none  [local(): lax.psum_scatter(v, 'seq', scatter_dimension=0, tiled=True)]
    pallas_call x2, Pallas kernels: 73.3 us -> 136 us  [the longest x1 123 us: attn_back_and_sums(): pl.pallas_call(functools.partial(back_kernel, sizes, table), in_specs=[an...]
    unnamed x1 -> x0, blocking collectives: 35.9 us -> none
    pallas_call x1, Pallas kernels: 44 us -> 28.9 us  [attn_fwd(): pl.pallas_call(attn_fwd_kernel, grid=(2,), in_specs=[pl.BlockSpec((HROWS,...]
  transfers between devices with their start and end apart: 8 -> 2, of which waited for: 4 -> 0; matrix products, arithmetic and copies ran while one was open for 2% -> 2% of each run, Pallas kernels for 23% -> 81%
where the time goes in v3:
time: 317 us; the launch traced here: 312 us
  Pallas kernels  275 us (87%)
  starting transfers between devices  13.6 us (4%)
  other arithmetic  11.6 us (4%)
  local copies, waits for them, and re-layouts  10.7 us (3%)
    pallas_call x1, Pallas kernels, attn_back_and_sums(): pl.pallas_call(functools.partial(back_kernel, sizes, table), in_specs=[an...  123 us
    pallas_call x1, Pallas kernels, mlp_bwd(): pl.pallas_call(mlp_bwd_kernel, grid=(FSTEPS,), in_specs=[whole((ROWS, DEC...  50.7 us
    pallas_call x1, Pallas kernels, mlp_fwd(): pl.pallas_call(mlp_fwd_kernel, grid=(FSTEPS,), in_specs=[whole((ROWS, D))...  39.3 us
    pallas_call x1, Pallas kernels, attn_fwd(): pl.pallas_call(attn_fwd_kernel, grid=(2,), in_specs=[pl.BlockSpec((HROWS,...  28.9 us
    pallas_call x1, Pallas kernels, finish(): pl.pallas_call(functools.partial(finish_kernel, seq_count, slots, table),...  12.7 us
    pallas_call x1, Pallas kernels, pick(): pl.pallas_call(functools.partial(pick_kernel, seq_count, slots), grid=(se...  8.94 us
    reduce_sum x1, other arithmetic, decoder_codes(): rank = jnp.sum(below.astype(jnp.int32), axis=0)  8.02 us
    all_to_all x1, starting transfers between devices, local(): lax.all_to_all(grad_slots, 'seq', split_axis=0, concat_axis=0, tiled=True)  7.63 us
  transfers between devices with their start and end apart: 2, of which 0 were waited for; matrix products, arithmetic and copies ran while one was open for 2% of the time, Pallas kernels for 81%

profile of v3, /device:TPU:0, one launch (start us, length us, event | category | flops | bytes accessed | tf_op | source)
XLA Modules:
  0.0 312.0 jit_solution(5377787846212063947)
XLA Ops:
  0.7 0.9 copy.49
  1.6 0.1 iota_add_fusion.1
  1.7 0.1 broadcast_compare_fusion
  1.8 8.0 %convert_reduce_fusion = (s32[8,28,32]{2,1,0:T(8,128)S(1)}, s32[8,28,32]{2,1,0:T(8,128)S(1)}) fusion(s32[8,28]{1,0:T(8,128)S(1)} %iota_add_fusion.1, s32[49,8,32]{0,2,1:T(8,128)S(1)} %bitcast.32, pred[49,8,32]{0,2,1:T(8,128)(4,1)S(1)} %broadcast_compare_fusion), kind=kLoop, calls=%fused_computation | loop fusion | flops 2444288 | bytes 120960 | tf_op jit(solution)/shard_map/reduce_sum | solution.py:1071
  9.8 0.1 mul.61
  10.0 0.1 gt.19
  10.1 0.1 add_compare_fusion
  10.2 0.1 broadcast_in_dim.20
  10.3 0.1 broadcast_in_dim.38
  10.4 0.1 add.140
  10.5 0.7 select_select_fusion.code_ref.refs_0_
  11.2 8.9 %pick.1 = (bf16[96,32,512]{2,1,0:T(8,128)(2,1)}, f32[8,512]{1,0:T(8,128)}) custom-call(s32[8,1,896]{2,1,0:T(1,128)} %select_select_fusion.code_ref.refs_0_, bf16[6272,512]{1,0:T(8,128)(2,1)} %dec_ref.1), custom_call_target="tpu_custom_call" | custom-call | tf_op jit(solution)/shard_map/pick/pallas_call | solution.py:121
  20.1 0.0 copy-start.9
  20.1 0.0 copy-start.10
  20.1 0.0 copy-start.5
  20.2 0.0 copy-start.6
  20.2 0.0 copy-start.7
  20.2 0.0 copy-start.8
  20.2 7.6 %all-to-all-start.1 = ((bf16[96,32,512]{2,1,0:T(8,128)(2,1)}), bf16[96,32,512]{2,1,0:T(8,128)(2,1)S(1)}, u32[]{:S(2)}, u32[]{:S(2)}) async-start(bf16[96,32,512]{2,1,0:T(8,128)(2,1)} %get-tuple-element.58), calls=%async_computation.1 | async-start | bytes 6291456 | tf_op jit(solution)/shard_map/all_to_all | solution.py:1118
  27.8 0.0 copy-done.2
  27.8 0.1 add_select_fusion
  27.9 0.1 copy.53
  28.0 1.1 convert_reduce_fusion.2
  29.2 0.1 multiply_add_fusion
  29.3 0.1 copy.54
  29.4 0.7 reshape.286.code_ref
  30.1 0.0 copy-done.3
  30.1 0.6 reshape.287.gain_ref.refs_9_
  30.6 0.6 reshape.288.shift_ref.refs_10_
  31.2 0.6 reshape.289.bias_ref
  31.8 0.6 reshape.290.obias_ref
  32.4 0.6 reshape.291.gain_ref
  33.0 0.6 reshape.292.shift_ref
  33.6 0.6 reshape.294.b2_ref
  34.2 28.9 %attn_fwd.1 = (bf16[3,32,64,768]{3,2,1,0:T(8,128)(2,1)}, bf16[1568,768]{1,0:T(8,128)(2,1)}, f32[1568,768]{1,0:T(8,128)}) custom-call(bf16[1568,768]{1,0:T(8,128)(2,1)} %refs_3_.1, f32[1,768]{1,0:T(1,128)} %reshape.287.gain_ref.refs_9_, f32[1,768]{1,0:T(1,128)} %reshape.288.shift_ref.refs_10_, bf16[768,2304]{1,0:T(8,128)(2,1)} %refs_5_.1, ...), custom_call_target="tpu_custom_call" | custom-call | tf_op jit(solution)/shard_map/attn_fwd/pallas_call | solution.py:275
  63.2 39.3 %mlp_fwd.1 = (bf16[1568,3072]{1,0:T(8,128)(2,1)}, bf16[1568,3072]{1,0:T(8,128)(2,1)}, bf16[1568,768]{1,0:T(8,128)(2,1)}, bf16[1568,512]{1,0:T(8,128)(2,1)}) custom-call(f32[1568,768]{1,0:T(8,128)} %get-tuple-element.56.hidden_ref, f32[1,768]{1,0:T(1,128)} %reshape.291.gain_ref, f32[1,768]{1,0:T(1,128)} %reshape.292.shift_ref, bf16[768,3072]{1,0:T(8,128)(2,1)} %w1_ref.3, ...), custom_call_target="tpu_custom_call" | custom-call | tf_op jit(solution)/shard_map/mlp_fwd/pallas_call | solution.py:336
  102.4 6.0 %pack.1 = bf16[96,32,512]{2,1,0:T(8,128)(2,1)} custom-call(s32[2,1,784]{2,1,0:T(1,128)} %reshape.286.code_ref, bf16[1568,512]{1,0:T(8,128)(2,1)} %get-tuple-element.57.rows_ref), custom_call_target="tpu_custom_call" | custom-call | tf_op jit(solution)/shard_map/pack/pallas_call | solution.py:169
  108.4 0.0 all-to-all-done.1.slots_ref
  108.4 6.0 %all-to-all-start = ((bf16[96,32,512]{2,1,0:T(8,128)(2,1)}), bf16[96,32,512]{2,1,0:T(8,128)(2,1)}, u32[]{:S(2)}, u32[]{:S(2)}) async-start(bf16[96,32,512]{2,1,0:T(8,128)(2,1)} %pack.1), calls=%async_computation | async-start | bytes 6291456 | tf_op jit(solution)/shard_map/all_to_all | solution.py:1129
  114.4 5.3 %unpack.1.egrad_ref = bf16[1568,512]{1,0:T(8,128)(2,1)} custom-call(s32[2,1,784]{2,1,0:T(1,128)} %reshape.286.code_ref, bf16[96,32,512]{2,1,0:T(8,128)(2,1)} %copy-done), custom_call_target="tpu_custom_call" | custom-call | tf_op jit(solution)/shard_map/unpack/pallas_call | solution.py:191
  119.7 50.7 %mlp_bwd.1 = (f32[1568,768]{1,0:T(8,128)}, bf16[768,512]{1,0:T(8,128)(2,1)}, f32[1,512]{1,0:T(1,128)}, bf16[3072,768]{1,0:T(8,128)(2,1)}, f32[1,768]{1,0:T(1,128...) custom-call(bf16[1568,512]{1,0:T(8,128)(2,1)} %unpack.1.egrad_ref, ...), custom_call_target="tpu_custom_call" | custom-call | tf_op jit(solution)/shard_map/mlp_bwd/pallas_call | solution.py:401
  170.4 123.2 %attn_back_and_sums.1 = (bf16[1568,768]{1,0:T(8,128)(2,1)}, f32[16,768]{1,0:T(8,128)}, bf16[4,96,384]{2,1,0:T(8,128)(2,1)}, bf16[4,96,384]{2,1,0:T(8,128)(2,1)},...) custom-call(f32[1568,768]{1,0:T(8,128)} %get-tuple-element.62.refs_0, ...), custom_call_target="tpu_custom_call" | custom-call | tf_op jit(solution)/shard_map/attn_back_and_sums/pallas_call | solution.py:959
  293.6 0.0 all-to-all-done.refs_1_
  293.7 12.7 %finish.1 = (bf16[6272,512]{1,0:T(8,128)(2,1)}, f32[384,768]{1,0:T(8,128)}, f32[96,3072]{1,0:T(8,128)}, f32[96,512]{1,0:T(8,128)}, f32[96,768]{1,0:T(8,128)}, /*...) custom-call(s32[8,1,896]{2,1,0:T(1,128)} %select_select_fusion.code_ref.refs_0_, ...), custom_call_target="tpu_custom_call" | custom-call | tf_op jit(solution)/shard_map/finish/pallas_call | solution.py:1042
  306.3 1.5 slice_bitcast_fusion.2
  307.9 1.3 slice_bitcast_fusion
  309.1 1.3 reduce
  310.4 1.4 copy.56
  (22 shorter events, 0.1 us)
Async XLA Ops:
  20.1 7.7 %copy-start.2 = (s32[256,49]{0,1:T(8,128)S(1)}, s32[256,49]{0,1:T(8,128)}, u32[]{:S(2)}) copy-start(s32[256,49]{0,1:T(8,128)} %param.20) | copy-start | bytes 150532
  20.1 9.9 %copy-start.3 = (f32[768]{0:T(1024)S(1)}, f32[768]{0:T(1024)}, u32[]{:S(2)}) copy-start(f32[768]{0:T(1024)} %param.21) | copy-start | bytes 9220
  20.1 10.5 %copy-start.4 = (f32[768]{0:T(1024)S(1)}, f32[768]{0:T(1024)}, u32[]{:S(2)}) copy-start(f32[768]{0:T(1024)} %param.22) | copy-start | bytes 9220
  20.1 11.1 %copy-start.9 = (f32[768]{0:T(1024)S(1)}, f32[768]{0:T(1024)}, u32[]{:S(2)}) copy-start(f32[768]{0:T(1024)} %param.25) | copy-start | bytes 9220
  20.1 11.1 %copy-start.10 = (f32[768]{0:T(1024)S(1)}, f32[768]{0:T(1024)}, u32[]{:S(2)}) copy-start(f32[768]{0:T(1024)} %param.24) | copy-start | bytes 9220
  20.1 11.7 %copy-start.5 = (f32[768]{0:T(1024)S(1)}, f32[768]{0:T(1024)}, u32[]{:S(2)}) copy-start(f32[768]{0:T(1024)} %param.27) | copy-start | bytes 9220
  20.2 12.3 %copy-start.6 = (f32[768]{0:T(1024)S(1)}, f32[768]{0:T(1024)}, u32[]{:S(2)}) copy-start(f32[768]{0:T(1024)} %param.28) | copy-start | bytes 9220
  20.2 12.9 %copy-start.7 = (f32[768]{0:T(1024)S(1)}, f32[768]{0:T(1024)}, u32[]{:S(2)}) copy-start(f32[768]{0:T(1024)} %param.29) | copy-start | bytes 9220
  20.2 13.5 %copy-start.8 = (f32[768]{0:T(1024)S(1)}, f32[768]{0:T(1024)}, u32[]{:S(2)}) copy-start(f32[768]{0:T(1024)} %param.33) | copy-start | bytes 9220
  20.2 88.2 %all-to-all-start.1 = ((bf16[96,32,512]{2,1,0:T(8,128)(2,1)}), bf16[96,32,512]{2,1,0:T(8,128)(2,1)S(1)}, u32[]{:S(2)}, u32[]{:S(2)}) async-start(bf16[96,32,512]{2,1,0:T(8,128)(2,1)} %get-tuple-element.58), calls=%async_computation.1 | async-start | bytes 6291456 | tf_op jit(solution)/shard_map/all_to_all | solution.py:1118
  108.4 6.0 %copy-start = (bf16[96,32,512]{2,1,0:T(8,128)(2,1)}, bf16[96,32,512]{2,1,0:T(8,128)(2,1)S(1)}, u32[]{:S(2)}) copy-start(bf16[96,32,512]{2,1,0:T(8,128)(2,1)S(1)} %all-to-all-done.1.slots_ref) | copy-start | bytes 9437188
  108.4 185.3 %all-to-all-start = ((bf16[96,32,512]{2,1,0:T(8,128)(2,1)}), bf16[96,32,512]{2,1,0:T(8,128)(2,1)}, u32[]{:S(2)}, u32[]{:S(2)}) async-start(bf16[96,32,512]{2,1,0:T(8,128)(2,1)} %pack.1), calls=%async_computation | async-start | bytes 6291456 | tf_op jit(solution)/shard_map/all_to_all | solution.py:1129
  293.6 16.8 %copy-start.1 = (bf16[1568,768]{1,0:T(8,128)(2,1)S(1)}, bf16[1568,768]{1,0:T(8,128)(2,1)}, u32[]{:S(2)}) copy-start(bf16[1568,768]{1,0:T(8,128)(2,1)} %get-tuple-element.127) | copy-start | bytes 7225348
